TPU v7x, 256 devices: a whole 4x4x8 slice. The times are simulated.
256 devices in a mesh: gx: 8 (over y, x_lo), gy: 32 (over z, x_hi, core).
Axes of the slice: x: 4 (x_hi: 2, x_lo: 2; x = x_hi * 2 + x_lo), y: 4, z: 8, core: 2. Of those that a mesh axis runs over, the one named last changes fastest.
Arguments:
- old_fields: float32 [4, 256, 512, 128], P(None, 'gx', 'gy'), may hold values from -12 to 12, as said below
- inverse_step: float32 [256, 512, 128], P('gx', 'gy'), may hold values from 8 to 64
- boundary: int32 [256, 512, 128], P('gx', 'gy'), may hold values from 0 to 1, as said below
Outputs:
- new_fields: float32 [4, 256, 512, 128], P(None, 'gx', 'gy')
- pressure: float32 [256, 512, 128], P('gx', 'gy')
Inputs may be any that keep to these rules, and one draw needn't show every extreme that they name: `old_fields`: drawn with a random sign and a magnitude that may vary over the brick. `boundary`: all copies of one mesh node hold the same value; the lowest node layer of every column and the top node plane are 0, and a column may have up to three fixed bottom layers.
All inputs are finite; a program needn't handle non-finite values.
Results may differ from a plain program's by a relative error of at most 0.00012.
Values sent between devices are 32-bit elements; how exact they have to be, the bound alone decides.
A program may use at most 64 MiB of HBM per device.

v0:
```python
import jax
import jax.numpy as jnp
import numpy as np
from jax import lax
from jax.sharding import PartitionSpec as P

ITERS = 6
CHEB = 6


SIGMA_SHIFT = 0.5
DIFFUSE = (1.0, 1.0, 1.0, 1.4)
COUPLING = 1.0
STRATIFY = 1.0
SPREAD = 20.0
HIGHEST_PRECISION = lax.Precision.HIGHEST
LOBATTO_POINTS = (
    -1.0,
    -0.8717401485096066,
    -0.5917001814331423,
    -0.2092992179024789,
    0.2092992179024789,
    0.5917001814331423,
    0.8717401485096066,
    1.0,
)


def extended(shard, sides, width):
    for axis, dim in sides:
        size, length = (lax.axis_size(axis), shard.shape[dim])
        up = [(i, (i + 1) % size) for i in range(size)]
        down = [(j, i) for i, j in up]
        last = lax.slice_in_dim(shard, length - width, length, axis=dim)
        leading = lax.slice_in_dim(shard, 0, width, axis=dim)
        before = lax.ppermute(last, axis, up)
        after = lax.ppermute(leading, axis, down)
        shard = jnp.concatenate([before, shard, after], axis=dim)
    return shard


def legendre_value(points, degree):
    previous = points * 0.0 + 1.0
    current = points
    for order in range(1, degree):
        following = ((2 * order + 1) * points * current - order * previous) / (order + 1)
        previous = current
        current = following
    return current


def quadrature_tables():
    degree = 7
    points = np.array(LOBATTO_POINTS)
    values = legendre_value(points, degree)
    weights = 2.0 / (degree * (degree + 1) * values * values)
    derive = np.zeros((degree + 1, degree + 1))
    for row_index in range(degree + 1):
        for column_index in range(degree + 1):
            if row_index != column_index:
                derive[row_index, column_index] = values[row_index] / (
                    values[column_index] * (points[row_index] - points[column_index])
                )
    derive[0, 0] = -degree * (degree + 1) / 4.0
    derive[degree, degree] = degree * (degree + 1) / 4.0
    stiffness_table = derive.T @ (weights[:, None] * derive)
    return (weights, derive, stiffness_table)


def node_lines(vector, extent_x, extent_y, extent_z):
    line_x = jnp.asarray(np.tile(vector, extent_x // 8), jnp.float32).reshape(extent_x, 1, 1)
    line_y = jnp.asarray(np.tile(vector, extent_y // 8), jnp.float32).reshape(extent_y, 1)
    line_z = jnp.asarray(np.tile(vector, extent_z // 8), jnp.float32)
    return (line_x, line_y, line_z)


def along_first(nodal, matrix):
    components, extent_x, extent_y, extent_z = nodal.shape
    blocks = nodal.reshape(components, extent_x // 8, 8, extent_y, extent_z)
    contracted = jnp.einsum(
        "ab,pebyz->peayz", jnp.asarray(matrix, jnp.float32), blocks, precision=HIGHEST_PRECISION
    )
    return contracted.reshape(nodal.shape)


def along_second(nodal, matrix):
    components, extent_x, extent_y, extent_z = nodal.shape
    blocks = nodal.reshape(components, extent_x, extent_y // 8, 8, extent_z)
    contracted = jnp.einsum(
        "ab,pxebz->pxeaz", jnp.asarray(matrix, jnp.float32), blocks, precision=HIGHEST_PRECISION
    )
    return contracted.reshape(nodal.shape)


def along_third(nodal, matrix):
    extent_z = nodal.shape[3]
    banded = jnp.asarray(np.kron(np.eye(extent_z // 8), matrix).T, jnp.float32)
    return jnp.matmul(nodal, banded, precision=HIGHEST_PRECISION)


def stiffness(nodal):
    weights, derive, stiffness_table = quadrature_tables()
    weight_x, weight_y, weight_z = node_lines(
        weights, nodal.shape[1], nodal.shape[2], nodal.shape[3]
    )
    total = along_first(nodal, stiffness_table) * weight_y * weight_z
    total = total + along_second(nodal, stiffness_table) * weight_x * weight_z
    return total + along_third(nodal, stiffness_table) * weight_x * weight_y


def pair_sum(nodal, dimension, preceding, following):
    length = nodal.shape[dimension]
    before = jnp.concatenate(
        [preceding, lax.slice_in_dim(nodal, 0, length - 1, axis=dimension)], axis=dimension
    )
    after_plane = jnp.concatenate(
        [lax.slice_in_dim(nodal, 1, length, axis=dimension), following], axis=dimension
    )
    layout = [1] * nodal.ndim
    layout[dimension] = length
    position = (jnp.arange(length) % 8).reshape(layout)
    return (
        nodal + jnp.where(position == 0, before, 0.0) + jnp.where(position == 7, after_plane, 0.0)
    )


def depth_sum(nodal):
    empty_plane = jnp.zeros_like(nodal[:, :, :, :1])
    return pair_sum(nodal, 3, empty_plane, empty_plane)


def periodic_assemble(nodal):
    nodal = pair_sum(nodal, 1, nodal[:, -1:], nodal[:, :1])
    nodal = pair_sum(nodal, 2, nodal[:, :, -1:], nodal[:, :, :1])
    return depth_sum(nodal)


def rim_sums(padded):
    summed = pair_sum(padded[:, 1:-1], 1, padded[:, :1], padded[:, -1:])
    return pair_sum(summed[:, :, 1:-1], 2, summed[:, :, :1], summed[:, :, -1:])


def assemble(nodal, family):
    if family == "velocity":
        padded = extended(nodal, (("gx", 1), ("gy", 2)), 1)
        nodal = rim_sums(padded)
    else:
        padded = extended(nodal, (("gx", 1), ("gy", 2)), 1)
        nodal = rim_sums(padded)
    return depth_sum(nodal)


def multiplicity_weights(extent_x, extent_y, extent_z):
    along_x = jnp.where(jnp.arange(extent_x) % 8 % 7 == 0, 0.5, 1.0).astype(jnp.float32)
    along_y = jnp.where(jnp.arange(extent_y) % 8 % 7 == 0, 0.5, 1.0).astype(jnp.float32)
    index_z = jnp.arange(extent_z)
    shared_z = (index_z % 8 % 7 == 0) & (index_z > 0) & (index_z < extent_z - 1)
    along_z = jnp.where(shared_z, 0.5, 1.0).astype(jnp.float32)
    return along_x.reshape(extent_x, 1, 1) * along_y.reshape(extent_y, 1) * along_z


def products(left_field, right_field, multiplicity):
    return jnp.sum(left_field * right_field * multiplicity, axis=(1, 2, 3))


def global_norm(nodal, multiplicity):
    return lax.psum(products(nodal, nodal, multiplicity), ("gx", "gy"))


def chebyshev_bounds():
    weights, derive, stiffness_table = quadrature_tables()
    weight_matrix = np.eye(8) * weights
    element_matrix = np.kron(np.kron(stiffness_table, weight_matrix), weight_matrix)
    element_matrix = element_matrix + np.kron(
        np.kron(weight_matrix, stiffness_table), weight_matrix
    )
    element_matrix = element_matrix + np.kron(
        np.kron(weight_matrix, weight_matrix), stiffness_table
    )
    element_matrix = element_matrix + SIGMA_SHIFT * np.kron(
        np.kron(weight_matrix, weight_matrix), weight_matrix
    )
    diagonal_index = np.arange(element_matrix.shape[0])
    bounds_ratio = (
        np.sum(np.abs(element_matrix), axis=1) / element_matrix[diagonal_index, diagonal_index]
    )
    upper_bound = float(np.max(bounds_ratio))
    lower_bound = upper_bound / SPREAD
    return ((upper_bound + lower_bound) / 2.0, (upper_bound - lower_bound) / 2.0)


def helmholtz(nodal, inverse_step, mass_weights, free_nodes, diffuse):
    return free_nodes * assemble(
        diffuse * stiffness(nodal) + inverse_step * mass_weights * nodal, "velocity"
    )


def on_device(old_fields, inverse_step, boundary):
    weights, derive, stiffness_table = quadrature_tables()
    free_nodes = boundary.astype(jnp.float32)
    extent_x, extent_y, extent_z = inverse_step.shape
    weight_x, weight_y, weight_z = node_lines(weights, extent_x, extent_y, extent_z)
    mass_weights = weight_x * weight_y * weight_z
    multiplicity = multiplicity_weights(extent_x, extent_y, extent_z)
    diffuse = jnp.asarray(np.array(DIFFUSE), jnp.float32).reshape(4, 1, 1, 1)
    nothing = jnp.zeros_like(old_fields[0])
    buoyancy = jnp.stack([nothing, nothing, COUPLING * old_fields[3], -STRATIFY * old_fields[2]])
    residual = free_nodes * assemble(
        mass_weights * (inverse_step * old_fields + buoyancy), "velocity"
    )
    solution = jnp.zeros_like(old_fields)
    direction = residual
    norm_now = global_norm(residual, multiplicity)
    for iteration in range(ITERS):
        applied = helmholtz(direction, inverse_step, mass_weights, free_nodes, diffuse)
        curvature = lax.psum(products(direction, applied, multiplicity), ("gx", "gy"))
        step_size = (norm_now / curvature).reshape(4, 1, 1, 1)
        solution = solution + step_size * direction
        residual = residual - step_size * applied
        norm_next = global_norm(residual, multiplicity)
        direction = residual + (norm_next / norm_now).reshape(4, 1, 1, 1) * direction
        norm_now = norm_next
    spread = (
        along_first(solution[0:1], derive)
        + along_second(solution[1:2], derive)
        + along_third(solution[2:3], derive)
    )
    source_term = -free_nodes * assemble(mass_weights * spread, "pressure")
    table_index = np.arange(8)
    diag_x, diag_y, diag_z = node_lines(
        stiffness_table[table_index, table_index], extent_x, extent_y, extent_z
    )
    local_diagonal = (
        diag_x * weight_y * weight_z
        + weight_x * diag_y * weight_z
        + weight_x * weight_y * diag_z
        + SIGMA_SHIFT * mass_weights
    )
    diagonal = periodic_assemble(local_diagonal[None])
    inverse = 1.0 / diagonal
    centre_value, half_width = chebyshev_bounds()
    factor = centre_value / half_width
    pressure = jnp.zeros_like(source_term)
    remainder = source_term
    update = inverse * remainder / centre_value
    damping = 1.0 / factor
    for iteration in range(CHEB):
        pressure = pressure + update
        if iteration < CHEB - 1:
            remainder = remainder - free_nodes * assemble(
                stiffness(update) + SIGMA_SHIFT * mass_weights * update, "pressure"
            )
            damping_next = 1.0 / (2.0 * factor - damping)
            update = (
                damping_next * damping * update
                + 2.0 * damping_next / half_width * inverse * remainder
            )
            damping = damping_next
    return (solution, pressure[0])


def solution(mesh):
    return jax.shard_map(
        on_device,
        mesh=mesh,
        in_specs=(P(None, "gx", "gy", None), P("gx", "gy", None), P("gx", "gy", None)),
        out_specs=(P(None, "gx", "gy", None), P("gx", "gy", None)),
        check_vma=False,
    )
```

profile of v0, /device:TPU:1, one launch (start us, length us, event | category | flops | bytes accessed | tf_op | source)
XLA Modules:
  0.0 1104.2 jit_solution(1860596041027865729)
XLA Ops:
  4.0 2.1 collective-permute-start
  6.1 2.5 collective-permute-start.1
  10.0 4.7 collective-permute-start.2
  16.0 4.6 collective-permute-done.3
  26.9 3.1 collective-permute-start.5
  33.9 4.1 collective-permute-done.7
  40.1 83.3 %all-reduce.28 = (f32[4]{0:T(128)S(1)}, f32[4]{0:T(128)S(1)}) all-reduce(f32[4]{0:T(128)S(1)} %get-tuple-element.3, f32[4]{0:T(128)S(1)} %get-tuple-element.2), channel_id=1, replica_groups=mesh['gx'=8,'gy'=32] {'gx','gy'}, use_global_device_ids=true, to_apply=%region_1.2 | all-reduce | flops 8 | bytes 64 | tf_op jit(solution)/shard_map/psum | solution.py:167
  123.7 72.4 %psum.86 = f32[4]{0:T(128)S(1)} all-reduce(f32[4]{0:T(128)S(1)} %multiply_reduce_fusion.9), channel_id=1, replica_groups=mesh['gx'=8,'gy'=32] {'gx','gy'}, use_global_device_ids=true, to_apply=%region_5.6 | all-reduce | flops 4 | bytes 32 | tf_op jit(solution)/shard_map/psum | solution.py:167
  196.2 1.4 multiply_add_fusion.5
  201.7 3.2 collective-permute-start.9
  206.3 3.0 collective-permute-start.10
  210.7 5.0 collective-permute-done.11
  216.9 1.7 multiply_reduce_fusion.8
  218.6 78.9 %psum.87 = f32[4]{0:T(128)S(1)} all-reduce(f32[4]{0:T(128)S(1)} %get-tuple-element.27), channel_id=1, replica_groups=mesh['gx'=8,'gy'=32] {'gx','gy'}, use_global_device_ids=true, to_apply=%region_7.8 | all-reduce | flops 4 | bytes 32 | tf_op jit(solution)/shard_map/psum | solution.py:216
  297.5 2.8 multiply_reduce_fusion.7
  300.3 72.4 %psum.88 = f32[4]{0:T(128)S(1)} all-reduce(f32[4]{0:T(128)S(1)} %get-tuple-element.25), channel_id=1, replica_groups=mesh['gx'=8,'gy'=32] {'gx','gy'}, use_global_device_ids=true, to_apply=%region_9.10 | all-reduce | flops 4 | bytes 32 | tf_op jit(solution)/shard_map/psum | solution.py:167
  373.2 1.4 multiply_add_fusion.4
  378.7 3.2 collective-permute-start.13
  383.4 3.0 collective-permute-start.14
  387.7 4.8 collective-permute-done.15
  394.3 2.2 multiply_reduce_fusion.6
  396.6 78.8 %psum.89 = f32[4]{0:T(128)} all-reduce(f32[4]{0:T(128)} %get-tuple-element.23), channel_id=1, replica_groups=mesh['gx'=8,'gy'=32] {'gx','gy'}, use_global_device_ids=true, to_apply=%region_11.12 | all-reduce | flops 4 | bytes 32 | tf_op jit(solution)/shard_map/psum | solution.py:216
  476.1 3.3 multiply_reduce_fusion.5
  479.4 72.5 %psum.90 = f32[4]{0:T(128)} all-reduce(f32[4]{0:T(128)} %get-tuple-element.21), channel_id=1, replica_groups=mesh['gx'=8,'gy'=32] {'gx','gy'}, use_global_device_ids=true, to_apply=%region_13.14 | all-reduce | flops 4 | bytes 32 | tf_op jit(solution)/shard_map/psum | solution.py:167
  552.5 1.4 multiply_add_fusion.3
  558.2 3.1 collective-permute-start.17
  562.8 2.9 collective-permute-start.18
  567.1 4.8 collective-permute-done.19
  573.8 2.2 multiply_reduce_fusion.4
  575.9 78.8 %psum.91 = f32[4]{0:T(128)} all-reduce(f32[4]{0:T(128)} %get-tuple-element.19), channel_id=1, replica_groups=mesh['gx'=8,'gy'=32] {'gx','gy'}, use_global_device_ids=true, to_apply=%region_15.16 | all-reduce | flops 4 | bytes 32 | tf_op jit(solution)/shard_map/psum | solution.py:216
  655.4 3.2 multiply_reduce_fusion.3
  658.7 72.5 %psum.92 = f32[4]{0:T(128)} all-reduce(f32[4]{0:T(128)} %get-tuple-element.17), channel_id=1, replica_groups=mesh['gx'=8,'gy'=32] {'gx','gy'}, use_global_device_ids=true, to_apply=%region_17.18 | all-reduce | flops 4 | bytes 32 | tf_op jit(solution)/shard_map/psum | solution.py:167
  731.8 1.7 multiply_add_fusion.2
  737.8 3.1 collective-permute-start.21
  742.4 3.0 collective-permute-start.22
  746.7 5.0 collective-permute-done.23
  753.5 2.2 multiply_reduce_fusion.2
  755.8 78.8 %psum.93 = f32[4]{0:T(128)} all-reduce(f32[4]{0:T(128)} %get-tuple-element.15), channel_id=1, replica_groups=mesh['gx'=8,'gy'=32] {'gx','gy'}, use_global_device_ids=true, to_apply=%region_19.20 | all-reduce | flops 4 | bytes 32 | tf_op jit(solution)/shard_map/psum | solution.py:216
  835.8 2.5 multiply_reduce_fusion.1
  838.3 1.6 fusion.174
  839.9 72.4 %psum.94 = f32[4]{0:T(128)} all-reduce(f32[4]{0:T(128)} %multiply_reduce_fusion.1), channel_id=1, replica_groups=mesh['gx'=8,'gy'=32] {'gx','gy'}, use_global_device_ids=true, to_apply=%region_21.22 | all-reduce | flops 4 | bytes 32 | tf_op jit(solution)/shard_map/psum | solution.py:167
  912.9 2.1 multiply_add_fusion.1
  919.3 3.1 collective-permute-start.25
  923.8 3.0 collective-permute-start.26
  928.1 4.8 collective-permute-done.27
  935.8 78.9 %psum.95 = f32[4]{0:T(128)S(1)} all-reduce(f32[4]{0:T(128)S(1)} %multiply_reduce_fusion), channel_id=1, replica_groups=mesh['gx'=8,'gy'=32] {'gx','gy'}, use_global_device_ids=true, to_apply=%region_23.24 | all-reduce | flops 4 | bytes 32 | tf_op jit(solution)/shard_map/psum | solution.py:216
  1014.8 2.3 multiply_add_fusion
  1018.5 3.6 collective-permute-start.29
  1023.2 3.0 collective-permute-start.30
  1027.0 4.1 collective-permute-done.31
  1034.0 3.6 collective-permute-start.33
  1039.5 1.7 collective-permute-start.35
  1041.6 3.0 collective-permute-done.35
  1046.8 3.6 collective-permute-start.37
  1051.4 1.5 collective-permute-start.38
  1052.9 3.3 collective-permute-start.39
  1056.8 1.6 collective-permute-done.39
  1060.7 3.6 collective-permute-start.41
  1065.3 1.4 collective-permute-start.42
  1066.8 4.5 collective-permute-start.43
  1074.7 3.9 collective-permute-start.45
  1080.8 5.7 collective-permute-start.47
  1089.5 4.0 collective-permute-start.49
  1094.6 6.8 collective-permute-start.51
  (322 shorter events, 95.0 us)
Async XLA Ops:
  3.7 196.4 %copy-start.11 = (f32[32,16,128]{2,1,0:T(8,128)}, f32[32,16,128]{2,1,0:T(8,128)S(1)}, u32[]{:S(2)}) copy-start(f32[32,16,128]{2,1,0:T(8,128)S(1)} %get-tuple-element.120) | copy-start | bytes 786436
  3.7 5.1 copy-start.9
  4.0 5.9 collective-permute-start
  6.1 3.8 collective-permute-start.1
  8.8 208.1 %copy-start.3 = (f32[32,16,128]{2,1,0:T(8,128)}, f32[32,16,128]{2,1,0:T(8,128)S(1)}, u32[]{:S(2)}) copy-start(f32[32,16,128]{2,1,0:T(8,128)S(1)} %convert_element_type.3) | copy-start | bytes 786436
  10.0 6.0 collective-permute-start.2
  14.7 6.0 collective-permute-start.3
  26.3 5.0 collective-permute-start.4
  26.9 4.4 collective-permute-start.5
  31.4 2.5 collective-permute-start.6
  32.5 5.4 collective-permute-start.7
  40.1 156.1 %copy-start.8 = (f32[4,32,16,128]{3,2,1,0:T(8,128)}, f32[4,32,16,128]{3,2,1,0:T(8,128)S(1)}, u32[]{:S(2)}) copy-start(f32[4,32,16,128]{3,2,1,0:T(8,128)S(1)} %get-tuple-element.29) | copy-start | bytes 3145732
  201.3 5.0 collective-permute-start.8
  201.7 4.5 collective-permute-start.9
  206.3 4.3 collective-permute-start.10
  209.3 6.3 collective-permute-start.11
  378.3 5.0 collective-permute-start.12
  378.7 4.5 collective-permute-start.13
  383.4 4.3 collective-permute-start.14
  386.3 6.1 collective-permute-start.15
  554.0 19.2 %copy-start = (f32[4,32,16,128]{3,2,1,0:T(8,128)}, f32[4,32,16,128]{3,2,1,0:T(8,128)S(1)}, u32[]{:S(2)}) copy-start(f32[4,32,16,128]{3,2,1,0:T(8,128)S(1)} %multiply_add_fusion.3) | copy-start | bytes 3145732
  557.7 5.0 collective-permute-start.16
  558.2 4.5 collective-permute-start.17
  562.8 4.3 collective-permute-start.18
  565.7 6.2 collective-permute-start.19
  733.6 19.4 %copy-start.1 = (f32[4,32,16,128]{3,2,1,0:T(8,128)}, f32[4,32,16,128]{3,2,1,0:T(8,128)S(1)}, u32[]{:S(2)}) copy-start(f32[4,32,16,128]{3,2,1,0:T(8,128)S(1)} %multiply_add_fusion.2) | copy-start | bytes 3145732
  737.3 5.0 collective-permute-start.20
  737.8 4.4 collective-permute-start.21
  742.4 4.3 collective-permute-start.22
  745.3 6.3 collective-permute-start.23
  915.0 19.1 %copy-start.2 = (f32[4,32,16,128]{3,2,1,0:T(8,128)}, f32[4,32,16,128]{3,2,1,0:T(8,128)S(1)}, u32[]{:S(2)}) copy-start(f32[4,32,16,128]{3,2,1,0:T(8,128)S(1)} %multiply_add_fusion.1) | copy-start | bytes 3145732
  918.7 5.0 collective-permute-start.24
  919.3 4.4 collective-permute-start.25
  923.8 4.3 collective-permute-start.26
  926.7 6.1 collective-permute-start.27
  934.8 80.0 %copy-start.39 = (f32[4]{0:T(128)S(1)}, f32[4]{0:T(128)}, u32[]{:S(2)}) copy-start(f32[4]{0:T(128)} %psum.94) | copy-start | bytes 52
  934.8 80.0 %copy-start.31 = (f32[4]{0:T(128)S(1)}, f32[4]{0:T(128)}, u32[]{:S(2)}) copy-start(f32[4]{0:T(128)} %copy-done.30) | copy-start | bytes 52
  934.8 80.0 %copy-start.34 = (f32[4]{0:T(128)S(1)}, f32[4]{0:T(128)}, u32[]{:S(2)}) copy-start(f32[4]{0:T(128)} %copy-done.33) | copy-start | bytes 52
  934.8 80.0 %copy-start.36 = (f32[4]{0:T(128)S(1)}, f32[4]{0:T(128)}, u32[]{:S(2)}) copy-start(f32[4]{0:T(128)} %copy-done.35) | copy-start | bytes 52
  934.8 80.0 %copy-start.38 = (f32[4]{0:T(128)S(1)}, f32[4]{0:T(128)}, u32[]{:S(2)}) copy-start(f32[4]{0:T(128)} %copy-done.37) | copy-start | bytes 52
  1018.4 4.7 collective-permute-start.28
  1018.5 4.6 collective-permute-start.29
  1023.2 3.8 collective-permute-start.30
  1026.1 5.0 collective-permute-start.31
  1033.9 4.7 collective-permute-start.32
  1034.0 4.6 collective-permute-start.33
  1038.6 3.0 collective-permute-start.34
  1039.5 5.0 collective-permute-start.35
  1046.7 4.7 collective-permute-start.36
  1046.8 4.6 collective-permute-start.37
  1051.4 5.4 collective-permute-start.38
  1052.9 5.5 collective-permute-start.39
  1060.6 4.7 collective-permute-start.40
  1060.7 4.6 collective-permute-start.41
  1065.3 6.5 collective-permute-start.42
  1066.8 5.5 collective-permute-start.43
  1074.3 5.2 collective-permute-start.44
  1074.7 4.8 collective-permute-start.45
  1079.5 7.5 collective-permute-start.46
  1080.8 6.5 collective-permute-start.47
  1089.4 5.1 collective-permute-start.48
  1089.5 5.0 collective-permute-start.49
  1094.5 7.5 collective-permute-start.50
  1094.6 7.7 collective-permute-start.51
  (29 other events, 49.0 us)
where the time goes:
time: 1120 us; the launch traced here: 1100 us
  blocking collectives  840 us (75%)
  starting transfers between devices  102 us (9%)
  waiting for transfers between devices  68.2 us (6%)
  other arithmetic  54.8 us (5%)
  matrix products  27.5 us (2%)
    psum x6, blocking collectives, global_norm(): return lax.psum(products(nodal, nodal, multiplicity), ('gx', 'gy'))  445 us
    psum x5, blocking collectives, on_device(): lax.psum(products(direction, applied, multiplicity), ('gx', 'gy'))  394 us
    ppermute x26, starting transfers between devices, extended(): after = lax.ppermute(leading, axis, down)  67.6 us
    ppermute x26, waiting for transfers between devices, extended(): after = lax.ppermute(leading, axis, down)  42.5 us
    ppermute x26, starting transfers between devices, extended(): before = lax.ppermute(last, axis, up)  34.7 us
    ppermute x26, waiting for transfers between devices, extended(): before = lax.ppermute(last, axis, up)  25.7 us
  transfers between devices with their start and end apart: 52, of which 39 were waited for; matrix products, arithmetic and copies ran while one was open for 0% of the time, Pallas kernels for 0%

commit v1 on v0

v1 whole, which is shorter than its diff:
```python
import jax
import jax.numpy as jnp
import ml_dtypes
import numpy as np
from jax import lax
from jax.experimental import pallas as pl
from jax.experimental.pallas import tpu as pltpu
from jax.sharding import PartitionSpec as P

ITERS = 6
CHEB = 6
SIGMA_SHIFT = 0.5
THERMAL = 1.4
COUPLING = 1.0
STRATIFY = 1.0
SPREAD = 20.0
CENTRE = 6.0
HALF = 2.9
LOBATTO_POINTS = (
    -1.0,
    -0.8717401485096066,
    -0.5917001814331423,
    -0.2092992179024789,
    0.2092992179024789,
    0.5917001814331423,
    0.8717401485096066,
    1.0,
)
MESH = pl.DeviceIdType.MESH
LX, LY, LZ = 32, 16, 128
ELEMENTS = LX // 8
F32 = jnp.float32
FACES = (
    (-1, 0, 0, 16, 16),
    (1, 0, 16, 0, 16),
    (0, -1, 32, 64, 32),
    (0, 1, 64, 32, 32),
    (-1, -1, 96, 120, 8),
    (-1, 1, 104, 112, 8),
    (1, -1, 112, 104, 8),
    (1, 1, 120, 96, 8),
)


def legendre_value(points, degree):
    previous = points * 0.0 + 1.0
    current = points
    for order in range(1, degree):
        following = ((2 * order + 1) * points * current - order * previous) / (order + 1)
        previous = current
        current = following
    return current


def quadrature_tables():
    degree = 7
    points = np.array(LOBATTO_POINTS)
    values = legendre_value(points, degree)
    weights = 2.0 / (degree * (degree + 1) * values * values)
    derive = np.zeros((degree + 1, degree + 1))
    for row in range(degree + 1):
        for column in range(degree + 1):
            if row != column:
                derive[row, column] = values[row] / (
                    values[column] * (points[row] - points[column])
                )
    derive[0, 0] = -degree * (degree + 1) / 4.0
    derive[degree, degree] = degree * (degree + 1) / 4.0
    return weights, derive, derive.T @ (weights[:, None] * derive)


def chebyshev_bounds():
    weights, _, stiff = quadrature_tables()
    w = np.diag(weights)
    element = np.kron(np.kron(stiff, w), w)
    element = element + np.kron(np.kron(w, stiff), w)
    element = element + np.kron(np.kron(w, w), stiff)
    element = element + SIGMA_SHIFT * np.kron(np.kron(w, w), w)
    upper = float(np.max(np.sum(np.abs(element), axis=1) / np.diag(element)))
    lower = upper / SPREAD
    return (upper + lower) / 2.0, (upper - lower) / 2.0


def chebyshev_coefficients():
    centre, half = chebyshev_bounds()
    ratio = centre / half
    damping = 1.0 / ratio
    pairs = [(0.0, 1.0 / centre)]
    for _ in range(CHEB - 1):
        following = 1.0 / (2.0 * ratio - damping)
        pairs.append((following * damping, 2.0 * following / half))
        damping = following
    return pairs


def split_pair(matrix):
    high = matrix.astype(ml_dtypes.bfloat16)
    low = (matrix - high.astype(np.float64)).astype(ml_dtypes.bfloat16)
    return high, low


def left_table(matrix):
    high, low = split_pair(matrix)
    return np.block([[high, high], [low, np.zeros_like(low)]])


def right_table(matrix):
    high, low = split_pair(matrix)
    return np.block([[high, low], [high, np.zeros_like(low)]])


def matrix_tables():
    weights, derive, stiff = quadrature_tables()
    scaled = stiff / weights[:, None]
    eye_y = np.eye(LY // 8)
    eye_z = np.eye(LZ // 8)
    lap_xy = np.kron(scaled, np.eye(LY)) + np.kron(np.eye(8), np.kron(eye_y, scaled))
    lap_z = np.kron(eye_z, scaled).T
    div_xy = np.concatenate(
        [np.kron(derive, np.eye(LY)), np.kron(np.eye(8), np.kron(eye_y, derive))], axis=1
    )
    div_z = np.kron(eye_z, derive).T
    return np.stack(
        [
            left_table(lap_xy),
            right_table(lap_z),
            np.concatenate(split_pair(div_xy), axis=0),
            right_table(div_z),
        ]
    )


def field_tables():
    weights, _, stiff = quadrature_tables()
    mass = weights[:, None, None] * np.tile(weights, 2)[None, :, None] * np.tile(weights, 16)
    shared = np.where(np.arange(8) % 7 == 0, 0.5, 1.0)
    shared_z = np.tile(shared, 16)
    shared_z[0] = shared_z[-1] = 1.0
    part = shared[:, None, None] * np.tile(shared, 2)[None, :, None] * shared_z

    def periodic(line):
        line = line.copy()
        line[0] = line[7] = line[0] + line[7]
        return line

    def column(line):
        line = np.tile(line, 16)
        total = line.copy()
        total[8::8] += line[7:-1:8]
        total[7:-1:8] += line[8::8]
        return total

    entry = np.diag(stiff)
    wx, sx = periodic(weights), periodic(entry)
    wy, sy = np.tile(wx, 2), np.tile(sx, 2)
    wz, sz = column(weights), column(entry)

    def outer(a, b, c):
        return a[:, None, None] * b[None, :, None] * c

    diagonal = outer(sx, wy, wz) + outer(wx, sy, wz) + outer(wx, wy, sz)
    diagonal = diagonal + SIGMA_SHIFT * outer(wx, wy, wz)
    return np.stack([mass / HALF, part, HALF / diagonal]).astype(np.float32)


def reduction_stages(nx, ny):
    bits_y = ny.bit_length() - 1
    bits = list(range(bits_y + nx.bit_length() - 1))
    stages = [[b for b in bits if b < 2 or b >= bits_y], [b for b in bits if 2 <= b < bits_y]]
    return [stage for stage in stages if stage]


def step_kernel(nx, ny, *refs):
    (old_hbm, inv_hbm, bnd_hbm, mat_ref, tab_ref, new_hbm, prs_hbm) = refs[:7]
    (old, inv, bnd, free, minv, basis, fields, rem, upd, prs) = refs[7:17]
    (vsnd, vrcv, psnd, prcv, macc, arow, arcv) = refs[17:24]
    (lsem, vss, vrs, pss, prs_sem, ass, ars, osem) = refs[24:]

    gx = lax.axis_index("gx")
    gy = lax.axis_index("gy")

    def neighbour(dx, dy):
        return (lax.rem(gx + dx + nx, nx), lax.rem(gy + dy + ny, ny))

    me = gx * ny + gy
    stages = []
    for bits in reduction_stages(nx, ny):
        partners = []
        for mask in range(1, 1 << len(bits)):
            other = me
            for place, b in enumerate(bits):
                if mask >> place & 1:
                    other = other + (1 - 2 * lax.rem(lax.div(me, 1 << b), 2)) * (1 << b)
            partners.append((mask, (lax.div(other, ny), lax.rem(other, ny))))
        stages.append(partners)

    loads = [
        pltpu.make_async_copy(inv_hbm, inv, lsem.at[0]),
        pltpu.make_async_copy(bnd_hbm, bnd, lsem.at[1]),
        pltpu.make_async_copy(old_hbm, old, lsem.at[2]),
    ]
    for load in loads:
        load.start()

    barrier = pltpu.get_barrier_semaphore()
    greeted = 0
    for dx, dy, *_ in FACES:
        pl.semaphore_signal(barrier, inc=1, device_id=neighbour(dx, dy), device_id_type=MESH)
        greeted += 1
    for partners in stages:
        for _, device in partners:
            pl.semaphore_signal(barrier, inc=1, device_id=device, device_id_type=MESH)
            greeted += 1

    lane = lax.broadcasted_iota(jnp.int32, (128, 128), 1)
    z_first = (lax.rem(lane, 8) == 0) & (lane > 0)
    z_last = (lax.rem(lane, 8) == 7) & (lane < LZ - 1)
    row3 = lax.broadcasted_iota(jnp.int32, (8, 8, 128), 1)
    row3_first, row3_last = row3 == 0, row3 == 7
    row = lax.broadcasted_iota(jnp.int32, (8, 128), 0)
    row_first, row_last = row == 0, row == 7
    tile_lane = lax.broadcasted_iota(jnp.int32, (8, 128), 1)

    def planes(e):
        return pl.ds(8 * e, 8)

    def inner_sums(w):
        flat = w.reshape(128, 128)
        flat = (
            flat
            + jnp.where(z_first, pltpu.roll(flat, 1, 1), 0.0)
            + jnp.where(z_last, pltpu.roll(flat, 127, 1), 0.0)
        )
        w = flat.reshape(8, LY, 128)
        a, b = w[:, :8], w[:, 8:]
        a_sum = a + jnp.where(row3_last, pltpu.roll(b, 7, 1), 0.0)
        b_sum = b + jnp.where(row3_first, pltpu.roll(a, 1, 1), 0.0)
        return jnp.concatenate([a_sum, b_sum], axis=1)

    def assembled(local, emit):
        before = None
        for e in range(ELEMENTS):
            w = inner_sums(local(e))
            if before is not None:
                both = before[7:] + w[:1]
                emit(e - 1, jnp.concatenate([before[:7], both], axis=0))
                w = jnp.concatenate([both, w[1:]], axis=0)
            before = w
        emit(ELEMENTS - 1, before)

    def pack(ref, e, w):
        ref[pl.ds(32 + 8 * e, 8), :] = w[:, 0, :]
        ref[pl.ds(64 + 8 * e, 8), :] = w[:, LY - 1, :]
        if e == 0:
            ref[pl.ds(0, 16), :] = w[0]
            ref[pl.ds(96, 1), :] = w[0, :1]
            ref[pl.ds(104, 1), :] = w[0, LY - 1 :]
        if e == ELEMENTS - 1:
            ref[pl.ds(16, 16), :] = w[7]
            ref[pl.ds(112, 1), :] = w[7, :1]
            ref[pl.ds(120, 1), :] = w[7, LY - 1 :]

    def spread_row(ref, r):
        return jnp.broadcast_to(ref[pl.ds(r, 1), :], (8, 128))

    def halo(ref, e):
        out = []
        for x in range(8):
            first = spread_row(ref, 32 + 8 * e + x)
            last = spread_row(ref, 64 + 8 * e + x)
            side = None
            if e == 0 and x == 0:
                side, corner = 0, 96
            if e == ELEMENTS - 1 and x == 7:
                side, corner = 16, 112
            if side is not None:
                first = first + spread_row(ref, corner)
                last = last + spread_row(ref, corner + 8)
            first = jnp.where(row_first, first, 0.0)
            last = jnp.where(row_last, last, 0.0)
            if side is not None:
                first = first + ref[pl.ds(side, 8), :]
                last = last + ref[pl.ds(side + 8, 8), :]
            out.append(jnp.concatenate([first, last], axis=0))
        return jnp.stack(out)

    def send_faces(src, dst, send_sem, recv_sem):
        for dx, dy, here, there, rows in FACES:
            pltpu.make_async_remote_copy(
                src_ref=src.at[pl.ds(here, rows)],
                dst_ref=dst.at[pl.ds(there, rows)],
                send_sem=send_sem,
                recv_sem=recv_sem,
                device_id=neighbour(dx, dy),
                device_id_type=MESH,
            ).start()

    def wait_all(ref, sem):
        pltpu.make_async_copy(ref, ref, sem).wait()

    def halves(v):
        high = v.astype(jnp.bfloat16)
        return high, (v - high.astype(F32)).astype(jnp.bfloat16)

    def along_z(high, low, index):
        out = jnp.dot(
            jnp.concatenate([high, low], axis=1), mat_ref[index], preferred_element_type=F32
        )
        return out[:, :128] + out[:, 128:]

    def laplace(v):
        high, low = halves(v)
        xy = jnp.dot(
            mat_ref[0], jnp.concatenate([high, low], axis=0), preferred_element_type=F32
        )
        return xy[:128] + xy[128:] + along_z(high, low, 1)

    mass, part, invd = tab_ref.at[0], tab_ref.at[1], tab_ref.at[2]

    def tile_sum(a):
        a = a.reshape(16, 8, 128)
        total = a[0]
        for k in range(1, 16):
            total = total + a[k]
        return total

    def record(slot, total):
        lanes = jnp.sum(total, axis=1, keepdims=True)
        macc[...] += jnp.where(tile_lane == slot, lanes, 0.0)

    loads[0].wait()
    loads[1].wait()
    macc[...] = jnp.zeros_like(macc)
    for e in range(ELEMENTS):
        free[planes(e)] = bnd[planes(e)].astype(F32)
        scaled = mass[...] * inv[planes(e)]
        minv[0, planes(e)] = scaled
        minv[1, planes(e)] = scaled * (1.0 / THERMAL)
        for c in range(4):
            basis[0, c, planes(e)] = jnp.zeros((8, LY, 128), F32)
    loads[2].wait()

    for c in range(4):

        def local_right(e, c=c):
            value = minv[0, planes(e)] * old[c, planes(e)]
            if c == 2:
                value = value + mass[...] * (COUPLING * old[3, planes(e)])
            if c == 3:
                value = value - mass[...] * (STRATIFY * old[2, planes(e)])
            return value

        def emit_right(e, w, c=c):
            basis[1, c, planes(e)] = free[planes(e)] * w
            pack(vsnd.at[0, c], e, w)

        assembled(local_right, emit_right)
        if c == 0:
            pl.semaphore_wait(barrier, greeted)
        send_faces(vsnd.at[0, c], vrcv.at[0, c], vss.at[0, c], vrs.at[0, c])

    shift = CENTRE / HALF

    def krylov(j, last):
        now = lax.rem(j, 2)
        later = 1 - now
        for c in range(4):
            wait_all(vrcv.at[now, c], vrs.at[now, c])
            totals = [jnp.zeros((8, 128), F32)] * 3
            if not last:

                @pl.when(j >= 1)
                def _(c=c):
                    wait_all(vsnd.at[later, c], vss.at[later, c])

            def local(e, c=c, totals=totals):
                v = basis[j + 1, c, planes(e)] + free[planes(e)] * halo(vrcv.at[now, c], e)
                basis[j + 1, c, planes(e)] = v
                weighted = v * part[...]
                totals[0] = totals[0] + tile_sum(weighted * v)
                totals[1] = totals[1] + tile_sum(weighted * basis[j, c, planes(e)])
                lap = laplace(v.reshape(128, 128)).reshape(8, LY, 128)
                w = mass[...] * lap + minv[c // 3, planes(e)] * v
                if last:
                    totals[2] = totals[2] + tile_sum(w * v)
                return w

            def emit(e, w, c=c):
                basis[j + 2, c, planes(e)] = (
                    free[planes(e)] * w
                    - shift * basis[j + 1, c, planes(e)]
                    - basis[j, c, planes(e)]
                )
                pack(vsnd.at[later, c], e, w)

            if last:
                for e in range(ELEMENTS):
                    local(e)
            else:
                assembled(local, emit)
                send_faces(
                    vsnd.at[later, c], vrcv.at[later, c], vss.at[later, c], vrs.at[later, c]
                )
            record(4 * j + c, totals[0])
            record(4 * (ITERS + j) + c, totals[1])
            if last:
                record(4 * 2 * ITERS + c, totals[2])

    def krylov_body(j, carry):
        krylov(j, False)
        return carry

    lax.fori_loop(0, ITERS - 1, krylov_body, 0)
    krylov(jnp.int32(ITERS - 1), True)

    value = jnp.sum(macc[...], axis=0, keepdims=True)
    for k, partners in enumerate(stages):
        arow[k] = value
        copies = []
        for mask, device in partners:
            copy = pltpu.make_async_remote_copy(
                src_ref=arow.at[k],
                dst_ref=arcv.at[k, mask],
                send_sem=ass.at[k, mask],
                recv_sem=ars.at[k, mask],
                device_id=device,
                device_id_type=MESH,
            )
            copy.start()
            copies.append(copy)
        for (mask, _), copy in zip(partners, copies):
            copy.wait_recv()
        for mask, _ in partners:
            value = value + arcv[k, mask]
        for copy in copies:
            copy.wait_send()

    def moment(index):
        return value if index == 0 else pltpu.roll(value, 128 - 4 * index, 1)

    q = [moment(j) for j in range(ITERS)]
    r = [moment(ITERS + j) for j in range(1, ITERS)]
    r.append(moment(2 * ITERS) - shift * q[-1] - r[-1])
    nu = []
    for j in range(ITERS):
        nu.append(q[j] - q[j - 1] if j else q[0])
        nu.append(r[j] - r[j - 1] if j else r[0])

    def gram(i, j):
        total = None
        for k in range(min(i, j) + 1):
            term = nu[abs(i - j) + 2 * k]
            total = term if total is None else total + term
        return total

    system = [[None] * ITERS for _ in range(ITERS)]
    for i in range(ITERS):
        for j in range(i, ITERS):
            entry = shift * gram(i, j) + gram(i, j + 1)
            if j:
                entry = entry + gram(i, j - 1)
            system[i][j] = entry
    right = [nu[i] for i in range(ITERS)]
    inverse = []
    for k in range(ITERS):
        inverse.append(1.0 / system[k][k])
        for i in range(k + 1, ITERS):
            factor = system[k][i] * inverse[k]
            for j in range(i, ITERS):
                system[i][j] = system[i][j] - factor * system[k][j]
            right[i] = right[i] - factor * right[k]
    answer = [None] * ITERS
    for k in reversed(range(ITERS)):
        total = right[k]
        for j in range(k + 1, ITERS):
            total = total - system[k][j] * answer[j]
        answer[k] = total * inverse[k]

    lane_row = lax.broadcasted_iota(jnp.int32, (1, 128), 1)
    for c in range(4):
        weights = []
        for j in range(ITERS):
            one = jnp.sum(jnp.where(lane_row == c, answer[j], 0.0), axis=1, keepdims=True)
            if c == 3:
                one = one * (1.0 / THERMAL)
            weights.append(jnp.broadcast_to(one, (8, 128)).reshape(1, 8, 128))
        for x in range(0, LX, 8):
            for y in range(0, LY, 8):
                where = (pl.ds(x, 8), pl.ds(y, 8))
                total = weights[0] * basis[1, c, where[0], where[1]]
                for j in range(1, ITERS):
                    total = total + weights[j] * basis[j + 1, c, where[0], where[1]]
                fields[c, where[0], where[1]] = total
    store_fields = pltpu.make_async_copy(fields, new_hbm, osem.at[0])
    store_fields.start()

    def local_source(e):
        u0, l0 = halves(fields[0, planes(e)].reshape(128, 128))
        u1, l1 = halves(fields[1, planes(e)].reshape(128, 128))
        u2, l2 = halves(fields[2, planes(e)].reshape(128, 128))
        high = jnp.dot(
            mat_ref[2], jnp.concatenate([u0, u1], axis=0), preferred_element_type=F32
        )
        low = jnp.dot(
            mat_ref[2, pl.ds(0, 128), :],
            jnp.concatenate([l0, l1], axis=0),
            preferred_element_type=F32,
        )
        total = high[:128] + high[128:] + low + along_z(u2, l2, 3)
        return mass[...] * total.reshape(8, LY, 128)

    def emit_source(e, w):
        rem[planes(e)] = -free[planes(e)] * w
        upd[planes(e)] = jnp.zeros((8, LY, 128), F32)
        prs[planes(e)] = jnp.zeros((8, LY, 128), F32)
        pack(psnd.at[0], e, w)

    assembled(local_source, emit_source)
    send_faces(psnd.at[0], prcv.at[0], pss.at[0], prs_sem.at[0])

    pairs = chebyshev_coefficients()

    def refreshed(e, now, keep, gain):
        left = rem[planes(e)] - free[planes(e)] * halo(prcv.at[now], e)
        update = keep * upd[planes(e)] + gain * (invd[...] * left)
        prs[planes(e)] = prs[planes(e)] + update
        return left, update

    def chebyshev_body(i, carry):
        now = lax.rem(i, 2)
        later = 1 - now
        keep, gain = jnp.float32(pairs[0][0]), jnp.float32(pairs[0][1])
        for k in range(1, CHEB - 1):
            keep = jnp.where(i == k, jnp.float32(pairs[k][0]), keep)
            gain = jnp.where(i == k, jnp.float32(pairs[k][1]), gain)
        wait_all(prcv.at[now], prs_sem.at[now])

        @pl.when(i >= 1)
        def _():
            wait_all(psnd.at[later], pss.at[later])

        def local(e):
            left, update = refreshed(e, now, keep, gain)
            rem[planes(e)] = left
            upd[planes(e)] = update
            lap = laplace(update.reshape(128, 128)).reshape(8, LY, 128)
            return mass[...] * (lap + SIGMA_SHIFT * update)

        def emit(e, w):
            rem[planes(e)] = rem[planes(e)] - free[planes(e)] * w
            pack(psnd.at[later], e, w)

        assembled(local, emit)
        send_faces(psnd.at[later], prcv.at[later], pss.at[later], prs_sem.at[later])
        return carry

    lax.fori_loop(0, CHEB - 1, chebyshev_body, 0)
    now = (CHEB - 1) % 2
    wait_all(prcv.at[now], prs_sem.at[now])
    for e in range(ELEMENTS):
        refreshed(e, now, pairs[CHEB - 1][0], pairs[CHEB - 1][1])
    store_pressure = pltpu.make_async_copy(prs, prs_hbm, osem.at[1])
    store_pressure.start()
    for slot in range(2):
        wait_all(psnd.at[slot], pss.at[slot])
        for c in range(4):
            wait_all(vsnd.at[slot, c], vss.at[slot, c])
    store_fields.wait()
    store_pressure.wait()


def solution(mesh):
    nx, ny = mesh.shape["gx"], mesh.shape["gy"]
    stages = reduction_stages(nx, ny)
    most = max(1 << len(bits) for bits in stages)
    matrices = matrix_tables()
    tables = field_tables()
    brick = (LX, LY, LZ)

    def body(*refs):
        step_kernel(nx, ny, *refs)

    def on_device(old_fields, inverse_step, boundary):
        any_space = pl.BlockSpec(memory_space=pl.ANY)
        vmem = pl.BlockSpec(memory_space=pltpu.VMEM)
        return pl.pallas_call(
            body,
            out_shape=(
                jax.ShapeDtypeStruct((4,) + brick, F32),
                jax.ShapeDtypeStruct(brick, F32),
            ),
            in_specs=[any_space] * 3 + [vmem] * 2,
            out_specs=(any_space, any_space),
            scratch_shapes=[
                pltpu.VMEM((4,) + brick, F32),
                pltpu.VMEM(brick, F32),
                pltpu.VMEM(brick, jnp.int32),
                pltpu.VMEM(brick, F32),
                pltpu.VMEM((2,) + brick, F32),
                pltpu.VMEM((ITERS + 1, 4) + brick, F32),
                pltpu.VMEM((4,) + brick, F32),
                pltpu.VMEM(brick, F32),
                pltpu.VMEM(brick, F32),
                pltpu.VMEM(brick, F32),
                pltpu.VMEM((2, 4, 128, 128), F32),
                pltpu.VMEM((2, 4, 128, 128), F32),
                pltpu.VMEM((2, 128, 128), F32),
                pltpu.VMEM((2, 128, 128), F32),
                pltpu.VMEM((8, 128), F32),
                pltpu.VMEM((len(stages), 1, 128), F32),
                pltpu.VMEM((len(stages), most, 1, 128), F32),
                pltpu.SemaphoreType.DMA((3,)),
                pltpu.SemaphoreType.DMA((2, 4)),
                pltpu.SemaphoreType.DMA((2, 4)),
                pltpu.SemaphoreType.DMA((2,)),
                pltpu.SemaphoreType.DMA((2,)),
                pltpu.SemaphoreType.DMA((len(stages), most)),
                pltpu.SemaphoreType.DMA((len(stages), most)),
                pltpu.SemaphoreType.DMA((2,)),
            ],
            compiler_params=pltpu.CompilerParams(
                collective_id=0, has_side_effects=True, vmem_limit_bytes=40 * 1024 * 1024
            ),
        )(old_fields, inverse_step, boundary, jnp.asarray(matrices), jnp.asarray(tables))

    return jax.shard_map(
        on_device,
        mesh=mesh,
        in_specs=(P(None, "gx", "gy", None), P("gx", "gy", None), P("gx", "gy", None)),
        out_specs=(P(None, "gx", "gy", None), P("gx", "gy", None)),
        check_vma=False,
    )
```

time: 1120 us -> 94.8 us (0.08); the launches traced: 1100 us -> 94.6 us
  blocking collectives: 840 us -> 0 us
  starting transfers between devices: 102 us -> 0 us
  Pallas kernels: 0 us -> 87.2 us
  waiting for transfers between devices: 68.2 us -> 0 us
  other arithmetic: 54.8 us -> 0 us
  matrix products: 27.5 us -> 0 us
    psum x11 -> x0, blocking collectives: 840 us -> none  [the longest x6 445 us: global_norm(): return lax.psum(products(nodal, nodal, multiplicity), ('gx', 'gy'))]
    ppermute x52 -> x0, starting transfers between devices: 102 us -> none  [the longest x26 67.6 us: extended(): after = lax.ppermute(leading, axis, down)]
    pallas_call x0 -> x1, Pallas kernels: none -> 87.2 us  [on_device(): pl.pallas_call(body, out_shape=(jax.ShapeDtypeStruct((4,) + brick, F32),...]
    ppermute x52 -> x0, waiting for transfers between devices: 68.2 us -> none  [the longest x26 42.5 us: extended(): after = lax.ppermute(leading, axis, down)]
    dot_general x36 -> x0, matrix products: 27.5 us -> none  [the longest x12 10 us: along_first(): jnp.einsum('ab,pebyz->peayz', jnp.asarray(matrix, jnp.float32), blocks, p...]
    reduce_sum x11 -> x0, other arithmetic: 22.2 us -> none  [products(): return jnp.sum(left_field * right_field * multiplicity, axis=(1, 2, 3))]
    add x38 -> x0, other arithmetic: 19.7 us -> none  [the longest x5 8.15 us: on_device(): residual + (norm_next / norm_now).reshape(4, 1, 1, 1) * direction]
  transfers between devices with their start and end apart: 52 -> 0, of which waited for: 39 -> 0; matrix products, arithmetic and copies ran while one was open for 0% -> 0% of each run, Pallas kernels for 0% -> 0%
where the time goes in v1:
time: 94.8 us; the launch traced here: 94.6 us
  Pallas kernels  87.2 us (92%)
  local copies, waits for them, and re-layouts  6.76 us (7%)
    pallas_call x1, Pallas kernels, on_device(): pl.pallas_call(body, out_shape=(jax.ShapeDtypeStruct((4,) + brick, F32),...  87.2 us
    unnamed x12, local copies, waits for them, and re-layouts  6.76 us

profile of v1, /device:TPU:1, one launch (start us, length us, event | category | flops | bytes accessed | tf_op | source)
XLA Modules:
  0.0 94.6 jit_solution(12185353113081765124)
XLA Ops:
  0.6 0.0 copy-start
  0.6 1.2 %copy-done = f32[4,32,16,128]{3,2,1,0:T(8,128)S(1)} copy-done((f32[4,32,16,128]{3,2,1,0:T(8,128)S(1)}, f32[4,32,16,128]{3,2,1,0:T(8,128)}, u32[]{:S(2)}) %copy-start) | copy-done | bytes 1048600
  1.9 0.0 copy-start.1
  1.9 1.0 %copy-done.1 = bf16[4,256,256]{2,1,0:T(8,128)(2,1)S(1)} copy-done((bf16[4,256,256]{2,1,0:T(8,128)(2,1)S(1)}, bf16[4,256,256]{2,1,0:T(8,128)(2,1)}, u32[]{:S(2)}) %copy-start.1) | copy-done | bytes 524312
  2.9 0.0 copy-start.2
  2.9 0.9 %copy-done.2 = f32[32,16,128]{2,1,0:T(8,128)S(1)} copy-done((f32[32,16,128]{2,1,0:T(8,128)S(1)}, f32[32,16,128]{2,1,0:T(8,128)}, u32[]{:S(2)}) %copy-start.2) | copy-done | bytes 262168
  3.8 0.0 copy-start.3
  3.9 0.9 %copy-done.3 = s32[32,16,128]{2,1,0:T(8,128)S(1)} copy-done((s32[32,16,128]{2,1,0:T(8,128)S(1)}, s32[32,16,128]{2,1,0:T(8,128)}, u32[]{:S(2)}) %copy-start.3) | copy-done | bytes 262168
  4.8 0.0 copy-start.4
  4.8 0.9 copy-done.4
  5.7 87.2 %shard_map.68 = (f32[4,32,16,128]{3,2,1,0:T(8,128)S(1)}, f32[32,16,128]{2,1,0:T(8,128)S(1)}) custom-call(f32[4,32,16,128]{3,2,1,0:T(8,128)S(1)} %copy-done, f32[32,16,128]{2,1,0:T(8,128)S(1)} %copy-done.2, s32[32,16,128]{2,1,0:T(8,128)S(1)} %copy-done.3, bf16[4,256,256]{2,1,0:T(8,128)(2,1)S(1)} %copy-done.1, f32[3,8,16,128]{3,2,1,0:T(8,128)S(1)} %copy-done.4), custom_call_target="tpu_custom_call" | custom-call | tf_op jit(solution)/shard_map/pallas_call | solution.py:586
  92.9 1.0 %copy.9 = f32[4,32,16,128]{3,2,1,0:T(8,128)} copy(f32[4,32,16,128]{3,2,1,0:T(8,128)S(1)} %get-tuple-element.4) | data formatting | bytes 2097152
  93.9 0.7 copy.10
Async XLA Ops:
  0.6 1.2 %copy-start = (f32[4,32,16,128]{3,2,1,0:T(8,128)S(1)}, f32[4,32,16,128]{3,2,1,0:T(8,128)}, u32[]{:S(2)}) copy-start(f32[4,32,16,128]{3,2,1,0:T(8,128)} %refs_0_.1) | copy-start | bytes 3145732
  1.9 1.0 %copy-start.1 = (bf16[4,256,256]{2,1,0:T(8,128)(2,1)S(1)}, bf16[4,256,256]{2,1,0:T(8,128)(2,1)}, u32[]{:S(2)}) copy-start(bf16[4,256,256]{2,1,0:T(8,128)(2,1)} %constant.4.clone.refs_3_) | copy-start | bytes 1572868
  2.9 0.9 %copy-start.2 = (f32[32,16,128]{2,1,0:T(8,128)S(1)}, f32[32,16,128]{2,1,0:T(8,128)}, u32[]{:S(2)}) copy-start(f32[32,16,128]{2,1,0:T(8,128)} %refs_1_.1) | copy-start | bytes 786436
  3.8 0.9 %copy-start.3 = (s32[32,16,128]{2,1,0:T(8,128)S(1)}, s32[32,16,128]{2,1,0:T(8,128)}, u32[]{:S(2)}) copy-start(s32[32,16,128]{2,1,0:T(8,128)} %refs_2_.1) | copy-start | bytes 786436
  4.8 0.9 copy-start.4

commit v2 on v1

--- a/solution.py
+++ b/solution.py
@@ -30,16 +30,10 @@
 LX, LY, LZ = 32, 16, 128
 ELEMENTS = LX // 8
 F32 = jnp.float32
-FACES = (
-    (-1, 0, 0, 16, 16),
-    (1, 0, 16, 0, 16),
-    (0, -1, 32, 64, 32),
-    (0, 1, 64, 32, 32),
-    (-1, -1, 96, 120, 8),
-    (-1, 1, 104, 112, 8),
-    (1, -1, 112, 104, 8),
-    (1, 1, 120, 96, 8),
-)
+X_FACES = ((-1, 0, 0, 16, 16), (1, 0, 16, 0, 16))
+Y_FACES = ((0, -1, 32, 64, 32), (0, 1, 64, 32, 32))
+FACE_ROWS = 96
+CORNERS = ((-1, -1, 0, 3), (-1, 1, 1, 2), (1, -1, 2, 1), (1, 1, 3, 0))
 
 
 def legendre_value(points, degree):
@@ -171,10 +165,11 @@
 
 
 def step_kernel(nx, ny, *refs):
-    (old_hbm, inv_hbm, bnd_hbm, mat_ref, tab_ref, new_hbm, prs_hbm) = refs[:7]
-    (old, inv, bnd, free, minv, basis, fields, rem, upd, prs) = refs[7:17]
-    (vsnd, vrcv, psnd, prcv, macc, arow, arcv) = refs[17:24]
-    (lsem, vss, vrs, pss, prs_sem, ass, ars, osem) = refs[24:]
+    (old_hbm, inv_hbm, bnd_hbm, mat_hbm, tab_hbm, new_hbm, prs_hbm) = refs[:7]
+    (old, inv, bnd, mat_ref, tab_ref, free, minv, basis, fields, rem, upd, prs) = refs[7:19]
+    (vsnd, vrcv, vcsnd, vcrcv, psnd, prcv, pcsnd, pcrcv) = refs[19:27]
+    (ssnd, srcv, scsnd, scrcv, hsum, hcsum, macc, arow, arcv) = refs[27:36]
+    (lsem, vsem, psem, ssem, ass, ars, osem) = refs[36:]
 
     gx = lax.axis_index("gx")
     gy = lax.axis_index("gy")
@@ -194,23 +189,25 @@
             partners.append((mask, (lax.div(other, ny), lax.rem(other, ny))))
         stages.append(partners)
 
-    loads = [
-        pltpu.make_async_copy(inv_hbm, inv, lsem.at[0]),
-        pltpu.make_async_copy(bnd_hbm, bnd, lsem.at[1]),
-        pltpu.make_async_copy(old_hbm, old, lsem.at[2]),
-    ]
-    for load in loads:
-        load.start()
-
     barrier = pltpu.get_barrier_semaphore()
     greeted = 0
-    for dx, dy, *_ in FACES:
+    for dx, dy, *_ in CORNERS + Y_FACES + X_FACES:
         pl.semaphore_signal(barrier, inc=1, device_id=neighbour(dx, dy), device_id_type=MESH)
         greeted += 1
     for partners in stages:
         for _, device in partners:
             pl.semaphore_signal(barrier, inc=1, device_id=device, device_id_type=MESH)
             greeted += 1
+
+    loads = [
+        pltpu.make_async_copy(inv_hbm, inv, lsem.at[0]),
+        pltpu.make_async_copy(bnd_hbm, bnd, lsem.at[1]),
+        pltpu.make_async_copy(tab_hbm, tab_ref, lsem.at[2]),
+        pltpu.make_async_copy(old_hbm, old, lsem.at[3]),
+        pltpu.make_async_copy(mat_hbm, mat_ref, lsem.at[4]),
+    ]
+    for load in loads:
+        load.start()
 
     lane = lax.broadcasted_iota(jnp.int32, (128, 128), 1)
     z_first = (lax.rem(lane, 8) == 0) & (lane > 0)
@@ -237,63 +234,125 @@
         b_sum = b + jnp.where(row3_first, pltpu.roll(a, 1, 1), 0.0)
         return jnp.concatenate([a_sum, b_sum], axis=1)
 
-    def assembled(local, emit):
-        before = None
-        for e in range(ELEMENTS):
-            w = inner_sums(local(e))
-            if before is not None:
-                both = before[7:] + w[:1]
-                emit(e - 1, jnp.concatenate([before[:7], both], axis=0))
-                w = jnp.concatenate([both, w[1:]], axis=0)
-            before = w
-        emit(ELEMENTS - 1, before)
-
-    def pack(ref, e, w):
-        ref[pl.ds(32 + 8 * e, 8), :] = w[:, 0, :]
-        ref[pl.ds(64 + 8 * e, 8), :] = w[:, LY - 1, :]
-        if e == 0:
-            ref[pl.ds(0, 16), :] = w[0]
-            ref[pl.ds(96, 1), :] = w[0, :1]
-            ref[pl.ds(104, 1), :] = w[0, LY - 1 :]
-        if e == ELEMENTS - 1:
-            ref[pl.ds(16, 16), :] = w[7]
-            ref[pl.ds(112, 1), :] = w[7, :1]
-            ref[pl.ds(120, 1), :] = w[7, LY - 1 :]
-
-    def spread_row(ref, r):
-        return jnp.broadcast_to(ref[pl.ds(r, 1), :], (8, 128))
-
-    def halo(ref, e):
+    def assembled(local, emit, ends=None, done=None):
+        w0 = inner_sums(local(0))
+        w3 = inner_sums(local(3))
+        if ends is not None:
+            ends(w0, w3)
+        w1 = inner_sums(local(1))
+        both = w0[7:] + w1[:1]
+        emit(0, jnp.concatenate([w0[:7], both], axis=0))
+        w1 = jnp.concatenate([both, w1[1:]], axis=0)
+        w2 = inner_sums(local(2))
+        both = w1[7:] + w2[:1]
+        emit(1, jnp.concatenate([w1[:7], both], axis=0))
+        w2 = jnp.concatenate([both, w2[1:]], axis=0)
+        both = w2[7:] + w3[:1]
+        emit(2, jnp.concatenate([w2[:7], both], axis=0))
+        emit(3, jnp.concatenate([both, w3[1:]], axis=0))
+        if done is not None:
+            done()
+
+    class Faces:
+        def __init__(self, send, receive, corner_send, corner_receive, sems):
+            self.send, self.receive = send, receive
+            self.corner_send, self.corner_receive = corner_send, corner_receive
+            self.sems = sems
+
+        def post(self, faces):
+            for dx, dy, here, there, rows in faces:
+                pltpu.make_async_remote_copy(
+                    src_ref=self.send.at[pl.ds(here, rows)],
+                    dst_ref=self.receive.at[pl.ds(there, rows)],
+                    send_sem=self.sems(0),
+                    recv_sem=self.sems(1),
+                    device_id=neighbour(dx, dy),
+                    device_id_type=MESH,
+                ).start()
+
+        def ends(self, w0, w3):
+            self.corner_send[0] = w0[0, :1]
+            self.corner_send[1] = w0[0, LY - 1 :]
+            self.corner_send[2] = w3[7, :1]
+            self.corner_send[3] = w3[7, LY - 1 :]
+            for dx, dy, here, there in CORNERS:
+                pltpu.make_async_remote_copy(
+                    src_ref=self.corner_send.at[here],
+                    dst_ref=self.corner_receive.at[there],
+                    send_sem=self.sems(2),
+                    recv_sem=self.sems(3),
+                    device_id=neighbour(dx, dy),
+                    device_id_type=MESH,
+                ).start()
+            self.send[pl.ds(0, 16), :] = w0[0]
+            self.send[pl.ds(16, 16), :] = w3[7]
+            self.post(X_FACES)
+
+        def rows(self, e, w):
+            self.send[pl.ds(32 + 8 * e, 8), :] = w[:, 0, :]
+            self.send[pl.ds(64 + 8 * e, 8), :] = w[:, LY - 1, :]
+
+        def done(self):
+            self.post(Y_FACES)
+
+        def arrived(self):
+            wait_all(self.receive, self.sems(1))
+            wait_all(self.corner_receive, self.sems(3))
+
+        def sent(self):
+            wait_all(self.send, self.sems(0))
+            wait_all(self.corner_send, self.sems(2))
+
+    def velocity_faces(slot, c):
+        return Faces(
+            vsnd.at[slot, c],
+            vrcv.at[slot, c],
+            vcsnd.at[slot, c],
+            vcrcv.at[slot, c],
+            lambda k: vsem.at[k, slot, c],
+        )
+
+    def pressure_faces(slot):
+        return Faces(
+            psnd.at[slot],
+            prcv.at[slot],
+            pcsnd.at[slot],
+            pcrcv.at[slot],
+            lambda k: psem.at[k, slot],
+        )
+
+    def source_faces(j, slot, c):
+        return Faces(
+            ssnd.at[slot, c],
+            srcv.at[j, c],
+            scsnd.at[slot, c],
+            scrcv.at[j, c],
+            lambda k: ssem.at[k, j, c],
+        )
+
+    def spread_row(line):
+        return jnp.broadcast_to(line, (8, 128))
+
+    def halo(faces, corners, e):
         out = []
         for x in range(8):
-            first = spread_row(ref, 32 + 8 * e + x)
-            last = spread_row(ref, 64 + 8 * e + x)
+            first = spread_row(faces[pl.ds(32 + 8 * e + x, 1), :])
+            last = spread_row(faces[pl.ds(64 + 8 * e + x, 1), :])
             side = None
             if e == 0 and x == 0:
-                side, corner = 0, 96
+                side, corner = 0, 0
             if e == ELEMENTS - 1 and x == 7:
-                side, corner = 16, 112
+                side, corner = 16, 2
             if side is not None:
-                first = first + spread_row(ref, corner)
-                last = last + spread_row(ref, corner + 8)
+                first = first + spread_row(corners[corner])
+                last = last + spread_row(corners[corner + 1])
             first = jnp.where(row_first, first, 0.0)
             last = jnp.where(row_last, last, 0.0)
             if side is not None:
-                first = first + ref[pl.ds(side, 8), :]
-                last = last + ref[pl.ds(side + 8, 8), :]
+                first = first + faces[pl.ds(side, 8), :]
+                last = last + faces[pl.ds(side + 8, 8), :]
             out.append(jnp.concatenate([first, last], axis=0))
         return jnp.stack(out)
-
-    def send_faces(src, dst, send_sem, recv_sem):
-        for dx, dy, here, there, rows in FACES:
-            pltpu.make_async_remote_copy(
-                src_ref=src.at[pl.ds(here, rows)],
-                dst_ref=dst.at[pl.ds(there, rows)],
-                send_sem=send_sem,
-                recv_sem=recv_sem,
-                device_id=neighbour(dx, dy),
-                device_id_type=MESH,
-            ).start()
 
     def wait_all(ref, sem):
         pltpu.make_async_copy(ref, ref, sem).wait()
@@ -328,8 +387,8 @@
         lanes = jnp.sum(total, axis=1, keepdims=True)
         macc[...] += jnp.where(tile_lane == slot, lanes, 0.0)
 
-    loads[0].wait()
-    loads[1].wait()
+    for load in loads[:3]:
+        load.wait()
     macc[...] = jnp.zeros_like(macc)
     for e in range(ELEMENTS):
         free[planes(e)] = bnd[planes(e)].astype(F32)
@@ -338,7 +397,7 @@
         minv[1, planes(e)] = scaled * (1.0 / THERMAL)
         for c in range(4):
             basis[0, c, planes(e)] = jnp.zeros((8, LY, 128), F32)
-    loads[2].wait()
+    loads[3].wait()
 
     for c in range(4):
 
@@ -350,31 +409,67 @@
                 value = value - mass[...] * (STRATIFY * old[2, planes(e)])
             return value
 
-        def emit_right(e, w, c=c):
+        faces = velocity_faces(0, c)
+
+        def emit_right(e, w, c=c, faces=faces):
             basis[1, c, planes(e)] = free[planes(e)] * w
-            pack(vsnd.at[0, c], e, w)
-
-        assembled(local_right, emit_right)
-        if c == 0:
-            pl.semaphore_wait(barrier, greeted)
-        send_faces(vsnd.at[0, c], vrcv.at[0, c], vss.at[0, c], vrs.at[0, c])
+            faces.rows(e, w)
+
+        def ends_right(w0, w3, c=c, faces=faces):
+            if c == 0:
+                pl.semaphore_wait(barrier, greeted)
+            faces.ends(w0, w3)
+
+        assembled(local_right, emit_right, ends_right, faces.done)
+    loads[4].wait()
 
     shift = CENTRE / HALF
+
+    def divergence(c, v):
+        high, low = halves(v)
+        if c == 2:
+            return along_z(high, low, 3)
+        out = jnp.dot(
+            mat_ref[2, :, pl.ds(128 * c, 128)], high, preferred_element_type=F32
+        )
+        low = jnp.dot(
+            mat_ref[2, pl.ds(0, 128), pl.ds(128 * c, 128)], low, preferred_element_type=F32
+        )
+        return out[:128] + out[128:] + low
+
+    def source_parts(j):
+        slot = lax.rem(j, 2)
+        for c in range(3):
+            faces = source_faces(j, slot, c)
+
+            @pl.when(j >= 2)
+            def _(c=c, slot=slot):
+                source_faces(j - 2, slot, c).sent()
+
+            def local(e, c=c):
+                v = basis[j + 1, c, planes(e)].reshape(128, 128)
+                return mass[...] * divergence(c, v).reshape(8, LY, 128)
+
+            assembled(local, faces.rows, faces.ends, faces.done)
 
     def krylov(j, last):
         now = lax.rem(j, 2)
         later = 1 - now
         for c in range(4):
-            wait_all(vrcv.at[now, c], vrs.at[now, c])
+            here = velocity_faces(now, c)
+            there = velocity_faces(later, c)
+            here.arrived()
             totals = [jnp.zeros((8, 128), F32)] * 3
             if not last:
 
                 @pl.when(j >= 1)
-                def _(c=c):
-                    wait_all(vsnd.at[later, c], vss.at[later, c])
-
-            def local(e, c=c, totals=totals):
-                v = basis[j + 1, c, planes(e)] + free[planes(e)] * halo(vrcv.at[now, c], e)
+                def _(there=there):
+                    there.sent()
+
+            def local(e, c=c, totals=totals, here=here):
+                v = basis[j + 1, c, planes(e)] + free[planes(e)] * halo(
+                    here.receive, here.corner_receive, e
+                )
                 basis[j + 1, c, planes(e)] = v
                 weighted = v * part[...]
                 totals[0] = totals[0] + tile_sum(weighted * v)
@@ -385,22 +480,19 @@
                     totals[2] = totals[2] + tile_sum(w * v)
                 return w
 
-            def emit(e, w, c=c):
+            def emit(e, w, c=c, there=there):
                 basis[j + 2, c, planes(e)] = (
                     free[planes(e)] * w
                     - shift * basis[j + 1, c, planes(e)]
                     - basis[j, c, planes(e)]
                 )
-                pack(vsnd.at[later, c], e, w)
+                there.rows(e, w)
 
             if last:
                 for e in range(ELEMENTS):
                     local(e)
             else:
-                assembled(local, emit)
-                send_faces(
-                    vsnd.at[later, c], vrcv.at[later, c], vss.at[later, c], vrs.at[later, c]
-                )
+                assembled(local, emit, there.ends, there.done)
             record(4 * j + c, totals[0])
             record(4 * (ITERS + j) + c, totals[1])
             if last:
@@ -408,6 +500,7 @@
 
     def krylov_body(j, carry):
         krylov(j, False)
+        source_parts(j)
         return carry
 
     lax.fori_loop(0, ITERS - 1, krylov_body, 0)
@@ -428,6 +521,8 @@
             )
             copy.start()
             copies.append(copy)
+        if k == 0:
+            source_parts(jnp.int32(ITERS - 1))
         for (mask, _), copy in zip(partners, copies):
             copy.wait_recv()
         for mask, _ in partners:
@@ -477,13 +572,17 @@
         answer[k] = total * inverse[k]
 
     lane_row = lax.broadcasted_iota(jnp.int32, (1, 128), 1)
-    for c in range(4):
-        weights = []
+
+    def coefficients(c):
+        out = []
         for j in range(ITERS):
             one = jnp.sum(jnp.where(lane_row == c, answer[j], 0.0), axis=1, keepdims=True)
             if c == 3:
                 one = one * (1.0 / THERMAL)
-            weights.append(jnp.broadcast_to(one, (8, 128)).reshape(1, 8, 128))
+            out.append(jnp.broadcast_to(one, (8, 128)).reshape(1, 8, 128))
+        return out
+
+    def combine(c, weights):
         for x in range(0, LX, 8):
             for y in range(0, LY, 8):
                 where = (pl.ds(x, 8), pl.ds(y, 8))
@@ -491,80 +590,105 @@
                 for j in range(1, ITERS):
                     total = total + weights[j] * basis[j + 1, c, where[0], where[1]]
                 fields[c, where[0], where[1]] = total
+
+    known = [coefficients(c) for c in range(3)]
+    for c in range(3):
+        combine(c, known[c])
+
+    for c in range(3):
+        for j in range(ITERS):
+            source_faces(j, j % 2, c).arrived()
+    for r in range(0, FACE_ROWS, 8):
+        total = None
+        for c in range(3):
+            for j in range(ITERS):
+                term = known[c][j][0] * srcv[j, c, pl.ds(r, 8), :]
+                total = term if total is None else total + term
+        hsum[pl.ds(r, 8), :] = total
+    for k in range(4):
+        total = None
+        for c in range(3):
+            for j in range(ITERS):
+                term = known[c][j][0, :1] * scrcv[j, c, k]
+                total = term if total is None else total + term
+        hcsum[k] = total
+
+    def local_source(e):
+        total = None
+        for c in range(3):
+            term = divergence(c, fields[c, planes(e)].reshape(128, 128))
+            total = term if total is None else total + term
+        return mass[...] * total.reshape(8, LY, 128)
+
+    pairs = chebyshev_coefficients()
+
+    def emit_source(e, w):
+        left = -free[planes(e)] * (w + halo(hsum, hcsum, e))
+        update = pairs[0][1] * (invd[...] * left)
+        rem[planes(e)] = left
+        upd[planes(e)] = update
+        prs[planes(e)] = update
+
+    assembled(local_source, emit_source)
+
+    def apply_pressure(local, faces):
+        def emit(e, w):
+            rem[planes(e)] = rem[planes(e)] - free[planes(e)] * w
+            faces.rows(e, w)
+
+        assembled(local, emit, faces.ends, faces.done)
+
+    def operator(update):
+        lap = laplace(update.reshape(128, 128)).reshape(8, LY, 128)
+        return mass[...] * (lap + SIGMA_SHIFT * update)
+
+    apply_pressure(lambda e: operator(upd[planes(e)]), pressure_faces(0))
+    combine(3, coefficients(3))
     store_fields = pltpu.make_async_copy(fields, new_hbm, osem.at[0])
     store_fields.start()
 
-    def local_source(e):
-        u0, l0 = halves(fields[0, planes(e)].reshape(128, 128))
-        u1, l1 = halves(fields[1, planes(e)].reshape(128, 128))
-        u2, l2 = halves(fields[2, planes(e)].reshape(128, 128))
-        high = jnp.dot(
-            mat_ref[2], jnp.concatenate([u0, u1], axis=0), preferred_element_type=F32
-        )
-        low = jnp.dot(
-            mat_ref[2, pl.ds(0, 128), :],
-            jnp.concatenate([l0, l1], axis=0),
-            preferred_element_type=F32,
-        )
-        total = high[:128] + high[128:] + low + along_z(u2, l2, 3)
-        return mass[...] * total.reshape(8, LY, 128)
-
-    def emit_source(e, w):
-        rem[planes(e)] = -free[planes(e)] * w
-        upd[planes(e)] = jnp.zeros((8, LY, 128), F32)
-        prs[planes(e)] = jnp.zeros((8, LY, 128), F32)
-        pack(psnd.at[0], e, w)
-
-    assembled(local_source, emit_source)
-    send_faces(psnd.at[0], prcv.at[0], pss.at[0], prs_sem.at[0])
-
-    pairs = chebyshev_coefficients()
-
-    def refreshed(e, now, keep, gain):
-        left = rem[planes(e)] - free[planes(e)] * halo(prcv.at[now], e)
+    def refreshed(e, faces, keep, gain):
+        left = rem[planes(e)] - free[planes(e)] * halo(faces.receive, faces.corner_receive, e)
         update = keep * upd[planes(e)] + gain * (invd[...] * left)
         prs[planes(e)] = prs[planes(e)] + update
         return left, update
 
     def chebyshev_body(i, carry):
-        now = lax.rem(i, 2)
-        later = 1 - now
-        keep, gain = jnp.float32(pairs[0][0]), jnp.float32(pairs[0][1])
-        for k in range(1, CHEB - 1):
+        now = lax.rem(i + 1, 2)
+        here = pressure_faces(now)
+        there = pressure_faces(1 - now)
+        keep, gain = jnp.float32(pairs[1][0]), jnp.float32(pairs[1][1])
+        for k in range(2, CHEB - 1):
             keep = jnp.where(i == k, jnp.float32(pairs[k][0]), keep)
             gain = jnp.where(i == k, jnp.float32(pairs[k][1]), gain)
-        wait_all(prcv.at[now], prs_sem.at[now])
-
-        @pl.when(i >= 1)
+        here.arrived()
+
+        @pl.when(i >= 2)
         def _():
-            wait_all(psnd.at[later], pss.at[later])
+            there.sent()
 
         def local(e):
-            left, update = refreshed(e, now, keep, gain)
+            left, update = refreshed(e, here, keep, gain)
             rem[planes(e)] = left
             upd[planes(e)] = update
-            lap = laplace(update.reshape(128, 128)).reshape(8, LY, 128)
-            return mass[...] * (lap + SIGMA_SHIFT * update)
-
-        def emit(e, w):
-            rem[planes(e)] = rem[planes(e)] - free[planes(e)] * w
-            pack(psnd.at[later], e, w)
-
-        assembled(local, emit)
-        send_faces(psnd.at[later], prcv.at[later], pss.at[later], prs_sem.at[later])
+            return operator(update)
+
+        apply_pressure(local, there)
         return carry
 
-    lax.fori_loop(0, CHEB - 1, chebyshev_body, 0)
-    now = (CHEB - 1) % 2
-    wait_all(prcv.at[now], prs_sem.at[now])
+    lax.fori_loop(1, CHEB - 1, chebyshev_body, 0)
+    here = pressure_faces(CHEB % 2)
+    here.arrived()
     for e in range(ELEMENTS):
-        refreshed(e, now, pairs[CHEB - 1][0], pairs[CHEB - 1][1])
+        refreshed(e, here, pairs[CHEB - 1][0], pairs[CHEB - 1][1])
     store_pressure = pltpu.make_async_copy(prs, prs_hbm, osem.at[1])
     store_pressure.start()
     for slot in range(2):
-        wait_all(psnd.at[slot], pss.at[slot])
+        pressure_faces(slot).sent()
         for c in range(4):
-            wait_all(vsnd.at[slot, c], vss.at[slot, c])
+            velocity_faces(slot, c).sent()
+        for c in range(3):
+            source_faces(ITERS - 2 + slot, slot, c).sent()
     store_fields.wait()
     store_pressure.wait()
 
@@ -582,19 +706,20 @@
 
     def on_device(old_fields, inverse_step, boundary):
         any_space = pl.BlockSpec(memory_space=pl.ANY)
-        vmem = pl.BlockSpec(memory_space=pltpu.VMEM)
         return pl.pallas_call(
             body,
             out_shape=(
                 jax.ShapeDtypeStruct((4,) + brick, F32),
                 jax.ShapeDtypeStruct(brick, F32),
             ),
-            in_specs=[any_space] * 3 + [vmem] * 2,
+            in_specs=[any_space] * 5,
             out_specs=(any_space, any_space),
             scratch_shapes=[
                 pltpu.VMEM((4,) + brick, F32),
                 pltpu.VMEM(brick, F32),
                 pltpu.VMEM(brick, jnp.int32),
+                pltpu.VMEM(matrices.shape, jnp.bfloat16),
+                pltpu.VMEM(tables.shape, F32),
                 pltpu.VMEM(brick, F32),
                 pltpu.VMEM((2,) + brick, F32),
                 pltpu.VMEM((ITERS + 1, 4) + brick, F32),
@@ -602,24 +727,33 @@
                 pltpu.VMEM(brick, F32),
                 pltpu.VMEM(brick, F32),
                 pltpu.VMEM(brick, F32),
-                pltpu.VMEM((2, 4, 128, 128), F32),
-                pltpu.VMEM((2, 4, 128, 128), F32),
-                pltpu.VMEM((2, 128, 128), F32),
-                pltpu.VMEM((2, 128, 128), F32),
+                pltpu.VMEM((2, 4, FACE_ROWS, 128), F32),
+                pltpu.VMEM((2, 4, FACE_ROWS, 128), F32),
+                pltpu.VMEM((2, 4, 4, 1, 128), F32),
+                pltpu.VMEM((2, 4, 4, 1, 128), F32),
+                pltpu.VMEM((2, FACE_ROWS, 128), F32),
+                pltpu.VMEM((2, FACE_ROWS, 128), F32),
+                pltpu.VMEM((2, 4, 1, 128), F32),
+                pltpu.VMEM((2, 4, 1, 128), F32),
+                pltpu.VMEM((2, 3, FACE_ROWS, 128), F32),
+                pltpu.VMEM((ITERS, 3, FACE_ROWS, 128), F32),
+                pltpu.VMEM((2, 3, 4, 1, 128), F32),
+                pltpu.VMEM((ITERS, 3, 4, 1, 128), F32),
+                pltpu.VMEM((FACE_ROWS, 128), F32),
+                pltpu.VMEM((4, 1, 128), F32),
                 pltpu.VMEM((8, 128), F32),
                 pltpu.VMEM((len(stages), 1, 128), F32),
                 pltpu.VMEM((len(stages), most, 1, 128), F32),
-                pltpu.SemaphoreType.DMA((3,)),
-                pltpu.SemaphoreType.DMA((2, 4)),
-                pltpu.SemaphoreType.DMA((2, 4)),
-                pltpu.SemaphoreType.DMA((2,)),
-                pltpu.SemaphoreType.DMA((2,)),
+                pltpu.SemaphoreType.DMA((5,)),
+                pltpu.SemaphoreType.DMA((4, 2, 4)),
+                pltpu.SemaphoreType.DMA((4, 2)),
+                pltpu.SemaphoreType.DMA((4, ITERS, 3)),
                 pltpu.SemaphoreType.DMA((len(stages), most)),
                 pltpu.SemaphoreType.DMA((len(stages), most)),
                 pltpu.SemaphoreType.DMA((2,)),
             ],
             compiler_params=pltpu.CompilerParams(
-                collective_id=0, has_side_effects=True, vmem_limit_bytes=40 * 1024 * 1024
+                collective_id=0, has_side_effects=True, vmem_limit_bytes=63 * 1024 * 1024
             ),
         )(old_fields, inverse_step, boundary, jnp.asarray(matrices), jnp.asarray(tables))
 

time: 94.8 us -> 85.2 us (0.90)
  Pallas kernels: 87.2 us -> 81.4 us
  local copies, waits for them, and re-layouts: 6.76 us -> 3.03 us
    pallas_call x1, Pallas kernels: 87.2 us -> 81.4 us  [on_device(): pl.pallas_call(body, out_shape=(jax.ShapeDtypeStruct((4,) + brick, F32),...]
    unnamed x12 -> x4, local copies, waits for them, and re-layouts: 6.76 us -> 3.03 us
where the time goes in v2:
time: 85.2 us; the launch traced here: 85.1 us
  Pallas kernels  81.4 us (96%)
  local copies, waits for them, and re-layouts  3.03 us (4%)
    pallas_call x1, Pallas kernels, on_device(): pl.pallas_call(body, out_shape=(jax.ShapeDtypeStruct((4,) + brick, F32),...  81.4 us
    unnamed x4, local copies, waits for them, and re-layouts  3.03 us

profile of v2, /device:TPU:1, one launch (start us, length us, event | category | flops | bytes accessed | tf_op | source)
XLA Modules:
  0.0 85.1 jit_solution(6422622613108724375)
XLA Ops:
  0.6 81.4 %shard_map.68 = (f32[4,32,16,128]{3,2,1,0:T(8,128)}, f32[32,16,128]{2,1,0:T(8,128)}) custom-call(f32[4,32,16,128]{3,2,1,0:T(8,128)} %refs_0_.1, f32[32,16,128]{2,1,0:T(8,128)} %refs_1_.1, s32[32,16,128]{2,1,0:T(8,128)} %refs_2_.1, bf16[4,256,256]{2,1,0:T(8,128)(2,1)} %constant.4.clone.refs_3_, f32[3,8,16,128]{3,2,1,0:T(8,128)} %constant.5.clone.refs_4_), custom_call_target="tpu_custom_call" | custom-call | tf_op jit(solution)/shard_map/pallas_call | solution.py:709
  82.0 0.0 copy-start
  82.0 2.3 %copy.9 = f32[4,32,16,128]{3,2,1,0:T(8,128)} copy(f32[4,32,16,128]{3,2,1,0:T(8,128)} %get-tuple-element.4) | data formatting | bytes 2097152
  84.4 0.0 copy-done
  84.4 0.7 copy.10
Async XLA Ops:
  82.0 2.3 %copy-start = (f32[32,16,128]{2,1,0:T(8,128)S(1)}, f32[32,16,128]{2,1,0:T(8,128)}, u32[]{:S(2)}) copy-start(f32[32,16,128]{2,1,0:T(8,128)} %get-tuple-element.5) | copy-start | bytes 786436

commit v3 on v2

--- a/solution.py
+++ b/solution.py
@@ -160,16 +160,17 @@
 def reduction_stages(nx, ny):
     bits_y = ny.bit_length() - 1
     bits = list(range(bits_y + nx.bit_length() - 1))
-    stages = [[b for b in bits if b < 2 or b >= bits_y], [b for b in bits if 2 <= b < bits_y]]
+    first = [b for b in bits if b == 1 or b >= bits_y]
+    stages = [first, [b for b in bits if b not in first]]
     return [stage for stage in stages if stage]
 
 
 def step_kernel(nx, ny, *refs):
-    (old_hbm, inv_hbm, bnd_hbm, mat_hbm, tab_hbm, new_hbm, prs_hbm) = refs[:7]
-    (old, inv, bnd, mat_ref, tab_ref, free, minv, basis, fields, rem, upd, prs) = refs[7:19]
-    (vsnd, vrcv, vcsnd, vcrcv, psnd, prcv, pcsnd, pcrcv) = refs[19:27]
-    (ssnd, srcv, scsnd, scrcv, hsum, hcsum, macc, arow, arcv) = refs[27:36]
-    (lsem, vsem, psem, ssem, ass, ars, osem) = refs[36:]
+    (old_hbm, inv_hbm, bnd_hbm, mat_hbm, tab_hbm, fields, prs) = refs[:7]
+    (old, inv, bnd, mat_ref, tab_ref, free, minv, basis, rem, upd) = refs[7:17]
+    (vsnd, vrcv, vcsnd, vcrcv, psnd, prcv, pcsnd, pcrcv) = refs[17:25]
+    (ssnd, srcv, scsnd, scrcv, hsum, hcsum, macc, arow, arcv) = refs[25:34]
+    (lsem, vsem, psem, ssem, ass, ars) = refs[34:]
 
     gx = lax.axis_index("gx")
     gy = lax.axis_index("gy")
@@ -178,10 +179,19 @@
         return (lax.rem(gx + dx + nx, nx), lax.rem(gy + dy + ny, ny))
 
     me = gx * ny + gy
+    bits_y = ny.bit_length() - 1
+
+    def hops(b):
+        if b < 2:
+            return 2 * b
+        return 1 << (b - 2) if b < bits_y else max(1, b - bits_y)
+
     stages = []
     for bits in reduction_stages(nx, ny):
         partners = []
-        for mask in range(1, 1 << len(bits)):
+        masks = range(1, 1 << len(bits))
+        masks = sorted(masks, key=lambda m: -sum(hops(b) for i, b in enumerate(bits) if m >> i & 1))
+        for mask in masks:
             other = me
             for place, b in enumerate(bits):
                 if mask >> place & 1:
@@ -259,33 +269,60 @@
             self.corner_send, self.corner_receive = corner_send, corner_receive
             self.sems = sems
 
+        def start(self, source, target, dx, dy, k):
+            pltpu.make_async_remote_copy(
+                src_ref=source,
+                dst_ref=target,
+                send_sem=self.sems(k),
+                recv_sem=self.sems(k + 1),
+                device_id=neighbour(dx, dy),
+                device_id_type=MESH,
+            ).start()
+
         def post(self, faces):
             for dx, dy, here, there, rows in faces:
-                pltpu.make_async_remote_copy(
-                    src_ref=self.send.at[pl.ds(here, rows)],
-                    dst_ref=self.receive.at[pl.ds(there, rows)],
-                    send_sem=self.sems(0),
-                    recv_sem=self.sems(1),
-                    device_id=neighbour(dx, dy),
-                    device_id_type=MESH,
-                ).start()
-
-        def ends(self, w0, w3):
+                here, there = pl.ds(here, rows), pl.ds(there, rows)
+                if len(self.send.shape) == 3:
+                    source, target = self.send.at[:, here], self.receive.at[:, there]
+                else:
+                    source, target = self.send.at[here], self.receive.at[there]
+                self.start(source, target, dx, dy, 0)
+
+        def post_corners(self):
+            for dx, dy, here, there in CORNERS:
+                if len(self.send.shape) == 3:
+                    source, target = self.corner_send.at[:, here], self.corner_receive.at[:, there]
+                else:
+                    source, target = self.corner_send.at[here], self.corner_receive.at[there]
+                self.start(source, target, dx, dy, 2)
+
+        def field(self, c):
+            return Faces(
+                self.send.at[c],
+                self.receive.at[c],
+                self.corner_send.at[c],
+                self.corner_receive.at[c],
+                self.sems,
+            )
+
+        def keep_corners(self, w0, w3):
             self.corner_send[0] = w0[0, :1]
             self.corner_send[1] = w0[0, LY - 1 :]
             self.corner_send[2] = w3[7, :1]
             self.corner_send[3] = w3[7, LY - 1 :]
-            for dx, dy, here, there in CORNERS:
-                pltpu.make_async_remote_copy(
-                    src_ref=self.corner_send.at[here],
-                    dst_ref=self.corner_receive.at[there],
-                    send_sem=self.sems(2),
-                    recv_sem=self.sems(3),
-                    device_id=neighbour(dx, dy),
-                    device_id_type=MESH,
-                ).start()
+
+        def keep_sides(self, w0, w3):
             self.send[pl.ds(0, 16), :] = w0[0]
             self.send[pl.ds(16, 16), :] = w3[7]
+
+        def keep_ends(self, w0, w3):
+            self.keep_corners(w0, w3)
+            self.keep_sides(w0, w3)
+
+        def ends(self, w0, w3):
+            self.keep_corners(w0, w3)
+            self.post_corners()
+            self.keep_sides(w0, w3)
             self.post(X_FACES)
 
         def rows(self, e, w):
@@ -294,6 +331,10 @@
 
         def done(self):
             self.post(Y_FACES)
+
+        def post_all(self):
+            self.post_corners()
+            self.post(Y_FACES + X_FACES)
 
         def arrived(self):
             wait_all(self.receive, self.sems(1))
@@ -321,13 +362,9 @@
             lambda k: psem.at[k, slot],
         )
 
-    def source_faces(j, slot, c):
+    def source_faces(j):
         return Faces(
-            ssnd.at[slot, c],
-            srcv.at[j, c],
-            scsnd.at[slot, c],
-            scrcv.at[j, c],
-            lambda k: ssem.at[k, j, c],
+            ssnd.at[j], srcv.at[j], scsnd.at[j], scrcv.at[j], lambda k: ssem.at[k, j]
         )
 
     def spread_row(line):
@@ -437,20 +474,23 @@
         )
         return out[:128] + out[128:] + low
 
+    pairs = chebyshev_coefficients()
+
+    def operator(update):
+        lap = laplace(update.reshape(128, 128)).reshape(8, LY, 128)
+        return mass[...] * (lap + SIGMA_SHIFT * update)
+
     def source_parts(j):
-        slot = lax.rem(j, 2)
+        group = source_faces(j)
         for c in range(3):
-            faces = source_faces(j, slot, c)
-
-            @pl.when(j >= 2)
-            def _(c=c, slot=slot):
-                source_faces(j - 2, slot, c).sent()
+            faces = group.field(c)
 
             def local(e, c=c):
-                v = basis[j + 1, c, planes(e)].reshape(128, 128)
-                return mass[...] * divergence(c, v).reshape(8, LY, 128)
-
-            assembled(local, faces.rows, faces.ends, faces.done)
+                v = basis[j + 1, c, planes(e)]
+                return mass[...] * divergence(c, v.reshape(128, 128)).reshape(8, LY, 128)
+
+            assembled(local, faces.rows, faces.keep_ends)
+        group.post_all()
 
     def krylov(j, last):
         now = lax.rem(j, 2)
@@ -500,6 +540,7 @@
 
     def krylov_body(j, carry):
         krylov(j, False)
+
         source_parts(j)
         return carry
 
@@ -595,9 +636,8 @@
     for c in range(3):
         combine(c, known[c])
 
-    for c in range(3):
-        for j in range(ITERS):
-            source_faces(j, j % 2, c).arrived()
+    for j in range(ITERS):
+        source_faces(j).arrived()
     for r in range(0, FACE_ROWS, 8):
         total = None
         for c in range(3):
@@ -620,8 +660,6 @@
             total = term if total is None else total + term
         return mass[...] * total.reshape(8, LY, 128)
 
-    pairs = chebyshev_coefficients()
-
     def emit_source(e, w):
         left = -free[planes(e)] * (w + halo(hsum, hcsum, e))
         update = pairs[0][1] * (invd[...] * left)
@@ -629,8 +667,6 @@
         upd[planes(e)] = update
         prs[planes(e)] = update
 
-    assembled(local_source, emit_source)
-
     def apply_pressure(local, faces):
         def emit(e, w):
             rem[planes(e)] = rem[planes(e)] - free[planes(e)] * w
@@ -638,14 +674,9 @@
 
         assembled(local, emit, faces.ends, faces.done)
 
-    def operator(update):
-        lap = laplace(update.reshape(128, 128)).reshape(8, LY, 128)
-        return mass[...] * (lap + SIGMA_SHIFT * update)
-
+    assembled(local_source, emit_source)
     apply_pressure(lambda e: operator(upd[planes(e)]), pressure_faces(0))
     combine(3, coefficients(3))
-    store_fields = pltpu.make_async_copy(fields, new_hbm, osem.at[0])
-    store_fields.start()
 
     def refreshed(e, faces, keep, gain):
         left = rem[planes(e)] - free[planes(e)] * halo(faces.receive, faces.corner_receive, e)
@@ -661,6 +692,7 @@
         for k in range(2, CHEB - 1):
             keep = jnp.where(i == k, jnp.float32(pairs[k][0]), keep)
             gain = jnp.where(i == k, jnp.float32(pairs[k][1]), gain)
+
         here.arrived()
 
         @pl.when(i >= 2)
@@ -681,16 +713,23 @@
     here.arrived()
     for e in range(ELEMENTS):
         refreshed(e, here, pairs[CHEB - 1][0], pairs[CHEB - 1][1])
-    store_pressure = pltpu.make_async_copy(prs, prs_hbm, osem.at[1])
-    store_pressure.start()
     for slot in range(2):
         pressure_faces(slot).sent()
         for c in range(4):
             velocity_faces(slot, c).sent()
-        for c in range(3):
-            source_faces(ITERS - 2 + slot, slot, c).sent()
-    store_fields.wait()
-    store_pressure.wait()
+    for j in range(ITERS):
+        source_faces(j).sent()
+
+
+def store_kernel(fields, pressure, new_hbm, prs_hbm, sems):
+    stores = [
+        pltpu.make_async_copy(fields, new_hbm, sems.at[0]),
+        pltpu.make_async_copy(pressure, prs_hbm, sems.at[1]),
+    ]
+    for store in stores:
+        store.start()
+    for store in stores:
+        store.wait()
 
 
 def solution(mesh):
@@ -706,14 +745,13 @@
 
     def on_device(old_fields, inverse_step, boundary):
         any_space = pl.BlockSpec(memory_space=pl.ANY)
-        return pl.pallas_call(
+        operands = (old_fields, inverse_step, boundary, jnp.asarray(matrices), jnp.asarray(tables))
+        operands = [pltpu.with_memory_space_constraint(x, pltpu.HBM) for x in operands]
+        results = pl.pallas_call(
             body,
-            out_shape=(
-                jax.ShapeDtypeStruct((4,) + brick, F32),
-                jax.ShapeDtypeStruct(brick, F32),
-            ),
+            out_shape=(pltpu.VMEM((4,) + brick, F32), pltpu.VMEM(brick, F32)),
             in_specs=[any_space] * 5,
-            out_specs=(any_space, any_space),
+            out_specs=(pl.BlockSpec(memory_space=pltpu.VMEM),) * 2,
             scratch_shapes=[
                 pltpu.VMEM((4,) + brick, F32),
                 pltpu.VMEM(brick, F32),
@@ -723,8 +761,6 @@
                 pltpu.VMEM(brick, F32),
                 pltpu.VMEM((2,) + brick, F32),
                 pltpu.VMEM((ITERS + 1, 4) + brick, F32),
-                pltpu.VMEM((4,) + brick, F32),
-                pltpu.VMEM(brick, F32),
                 pltpu.VMEM(brick, F32),
                 pltpu.VMEM(brick, F32),
                 pltpu.VMEM((2, 4, FACE_ROWS, 128), F32),
@@ -735,9 +771,9 @@
                 pltpu.VMEM((2, FACE_ROWS, 128), F32),
                 pltpu.VMEM((2, 4, 1, 128), F32),
                 pltpu.VMEM((2, 4, 1, 128), F32),
-                pltpu.VMEM((2, 3, FACE_ROWS, 128), F32),
                 pltpu.VMEM((ITERS, 3, FACE_ROWS, 128), F32),
-                pltpu.VMEM((2, 3, 4, 1, 128), F32),
+                pltpu.VMEM((ITERS, 3, FACE_ROWS, 128), F32),
+                pltpu.VMEM((ITERS, 3, 4, 1, 128), F32),
                 pltpu.VMEM((ITERS, 3, 4, 1, 128), F32),
                 pltpu.VMEM((FACE_ROWS, 128), F32),
                 pltpu.VMEM((4, 1, 128), F32),
@@ -747,15 +783,26 @@
                 pltpu.SemaphoreType.DMA((5,)),
                 pltpu.SemaphoreType.DMA((4, 2, 4)),
                 pltpu.SemaphoreType.DMA((4, 2)),
-                pltpu.SemaphoreType.DMA((4, ITERS, 3)),
+                pltpu.SemaphoreType.DMA((4, ITERS)),
                 pltpu.SemaphoreType.DMA((len(stages), most)),
                 pltpu.SemaphoreType.DMA((len(stages), most)),
-                pltpu.SemaphoreType.DMA((2,)),
             ],
             compiler_params=pltpu.CompilerParams(
-                collective_id=0, has_side_effects=True, vmem_limit_bytes=63 * 1024 * 1024
+                collective_id=0, has_side_effects=True, vmem_limit_bytes=40 * 1024 * 1024
             ),
-        )(old_fields, inverse_step, boundary, jnp.asarray(matrices), jnp.asarray(tables))
+        )(*operands)
+        results = [pltpu.with_memory_space_constraint(x, pltpu.VMEM) for x in results]
+        return pl.pallas_call(
+            store_kernel,
+            out_shape=(
+                jax.ShapeDtypeStruct((4,) + brick, F32),
+                jax.ShapeDtypeStruct(brick, F32),
+            ),
+            in_specs=[any_space] * 2,
+            out_specs=(any_space, any_space),
+            scratch_shapes=[pltpu.SemaphoreType.DMA((2,))],
+            compiler_params=pltpu.CompilerParams(vmem_limit_bytes=8 * 1024 * 1024),
+        )(*results)
 
     return jax.shard_map(
         on_device,

time: 85.2 us -> 81.3 us (0.954)
  local copies, waits for them, and re-layouts: 3.03 us -> 0 us
    unnamed x4 -> x0, local copies, waits for them, and re-layouts: 3.03 us -> none
    pallas_call x1 -> x2, Pallas kernels: 81.4 us -> 80.6 us  [the longest x1 79.5 us: on_device(): pl.pallas_call(body, out_shape=(pltpu.VMEM((4,) + brick, F32), pltpu.VMEM...]
where the time goes in v3:
time: 81.3 us; the launch traced here: 81.2 us
  Pallas kernels  80.6 us (99%)
    pallas_call x1, Pallas kernels, on_device(): pl.pallas_call(body, out_shape=(pltpu.VMEM((4,) + brick, F32), pltpu.VMEM...  79.5 us

profile of v3, /device:TPU:1, one launch (start us, length us, event | category | flops | bytes accessed | tf_op | source)
XLA Modules:
  0.0 81.2 jit_solution(13365384953016534681)
XLA Ops:
  0.6 79.5 %shard_map.68 = (f32[4,32,16,128]{3,2,1,0:T(8,128)S(1)}, f32[32,16,128]{2,1,0:T(8,128)S(1)}) custom-call(f32[4,32,16,128]{3,2,1,0:T(8,128)} %refs_0_.1, f32[32,16,128]{2,1,0:T(8,128)} %refs_1_.1, s32[32,16,128]{2,1,0:T(8,128)} %refs_2_.1, bf16[4,256,256]{2,1,0:T(8,128)(2,1)} %constant.4.clone.refs_3_, f32[3,8,16,128]{3,2,1,0:T(8,128)} %constant.5.clone.refs_4_), custom_call_target="tpu_custom_call" | custom-call | tf_op jit(solution)/shard_map/pallas_call | solution.py:750
  80.1 1.1 %shard_map.69 = (f32[4,32,16,128]{3,2,1,0:T(8,128)}, f32[32,16,128]{2,1,0:T(8,128)}) custom-call(f32[4,32,16,128]{3,2,1,0:T(8,128)S(1)} %get-tuple-element.4.fields, f32[32,16,128]{2,1,0:T(8,128)S(1)} %get-tuple-element.5.pressure), custom_call_target="tpu_custom_call" | custom-call | tf_op jit(solution)/shard_map/pallas_call | solution.py:795

commit v4 on v3

--- a/solution.py
+++ b/solution.py
@@ -244,16 +244,18 @@
         b_sum = b + jnp.where(row3_first, pltpu.roll(a, 1, 1), 0.0)
         return jnp.concatenate([a_sum, b_sum], axis=1)
 
-    def assembled(local, emit, ends=None, done=None):
-        w0 = inner_sums(local(0))
-        w3 = inner_sums(local(3))
+    def assembled(local, emit, ends=None, done=None, gate=None):
+        if gate is not None:
+            w1, w2 = [inner_sums(w) for w in local((1, 2))]
+            gate()
+        w0, w3 = [inner_sums(w) for w in local((0, 3))]
         if ends is not None:
             ends(w0, w3)
-        w1 = inner_sums(local(1))
+        if gate is None:
+            w1, w2 = [inner_sums(w) for w in local((1, 2))]
         both = w0[7:] + w1[:1]
         emit(0, jnp.concatenate([w0[:7], both], axis=0))
         w1 = jnp.concatenate([both, w1[1:]], axis=0)
-        w2 = inner_sums(local(2))
         both = w1[7:] + w2[:1]
         emit(1, jnp.concatenate([w1[:7], both], axis=0))
         w2 = jnp.concatenate([both, w2[1:]], axis=0)
@@ -338,6 +340,12 @@
 
         def arrived(self):
             wait_all(self.receive, self.sems(1))
+            wait_all(self.corner_receive, self.sems(3))
+
+        def faces_arrived(self):
+            wait_all(self.receive, self.sems(1))
+
+        def corners_arrived(self):
             wait_all(self.corner_receive, self.sems(3))
 
         def sent(self):
@@ -398,18 +406,30 @@
         high = v.astype(jnp.bfloat16)
         return high, (v - high.astype(F32)).astype(jnp.bfloat16)
 
-    def along_z(high, low, index):
+    def along_z(highs, lows, index):
+        rows = [jnp.concatenate([h, l], axis=1) for h, l in zip(highs, lows)]
         out = jnp.dot(
-            jnp.concatenate([high, low], axis=1), mat_ref[index], preferred_element_type=F32
+            jnp.concatenate(rows, axis=0), mat_ref[index], preferred_element_type=F32
         )
-        return out[:, :128] + out[:, 128:]
-
-    def laplace(v):
-        high, low = halves(v)
-        xy = jnp.dot(
-            mat_ref[0], jnp.concatenate([high, low], axis=0), preferred_element_type=F32
+        out = out[:, :128] + out[:, 128:]
+        return [out[:128], out[128:]]
+
+    def split_blocks(blocks):
+        pairs = [halves(v.reshape(128, 128)) for v in blocks]
+        return [p[0] for p in pairs], [p[1] for p in pairs]
+
+    def laplace(blocks):
+        highs, lows = split_blocks(blocks)
+        stacked = jnp.concatenate(
+            [jnp.concatenate(highs, axis=1), jnp.concatenate(lows, axis=1)], axis=0
         )
-        return xy[:128] + xy[128:] + along_z(high, low, 1)
+        xy = jnp.dot(mat_ref[0], stacked, preferred_element_type=F32)
+        xy = xy[:128] + xy[128:]
+        z = along_z(highs, lows, 1)
+        return [
+            (xy[:, :128] + z[0]).reshape(8, LY, 128),
+            (xy[:, 128:] + z[1]).reshape(8, LY, 128),
+        ]
 
     mass, part, invd = tab_ref.at[0], tab_ref.at[1], tab_ref.at[2]
 
@@ -457,37 +477,39 @@
                 pl.semaphore_wait(barrier, greeted)
             faces.ends(w0, w3)
 
-        assembled(local_right, emit_right, ends_right, faces.done)
+        assembled(lambda es, f=local_right: [f(e) for e in es], emit_right, ends_right, faces.done)
     loads[4].wait()
 
     shift = CENTRE / HALF
 
-    def divergence(c, v):
-        high, low = halves(v)
+    def divergence(c, blocks):
+        highs, lows = split_blocks(blocks)
         if c == 2:
-            return along_z(high, low, 3)
-        out = jnp.dot(
-            mat_ref[2, :, pl.ds(128 * c, 128)], high, preferred_element_type=F32
-        )
-        low = jnp.dot(
-            mat_ref[2, pl.ds(0, 128), pl.ds(128 * c, 128)], low, preferred_element_type=F32
-        )
-        return out[:128] + out[128:] + low
+            out = along_z(highs, lows, 3)
+        else:
+            table = mat_ref[2, :, pl.ds(128 * c, 128)]
+            high = jnp.dot(table, jnp.concatenate(highs, axis=1), preferred_element_type=F32)
+            low = jnp.dot(
+                table[:128], jnp.concatenate(lows, axis=1), preferred_element_type=F32
+            )
+            total = high[:128] + high[128:] + low
+            out = [total[:, :128], total[:, 128:]]
+        return [block.reshape(8, LY, 128) for block in out]
 
     pairs = chebyshev_coefficients()
 
-    def operator(update):
-        lap = laplace(update.reshape(128, 128)).reshape(8, LY, 128)
-        return mass[...] * (lap + SIGMA_SHIFT * update)
+    def operator(updates):
+        laps = laplace(updates)
+        return [mass[...] * (lap + SIGMA_SHIFT * u) for lap, u in zip(laps, updates)]
 
     def source_parts(j):
         group = source_faces(j)
         for c in range(3):
             faces = group.field(c)
 
-            def local(e, c=c):
-                v = basis[j + 1, c, planes(e)]
-                return mass[...] * divergence(c, v.reshape(128, 128)).reshape(8, LY, 128)
+            def local(es, c=c):
+                blocks = [basis[j + 1, c, planes(e)] for e in es]
+                return [mass[...] * out for out in divergence(c, blocks)]
 
             assembled(local, faces.rows, faces.keep_ends)
         group.post_all()
@@ -498,7 +520,11 @@
         for c in range(4):
             here = velocity_faces(now, c)
             there = velocity_faces(later, c)
-            here.arrived()
+            gate = here.corners_arrived if c == 0 and not last else None
+            if gate is None:
+                here.arrived()
+            else:
+                here.faces_arrived()
             totals = [jnp.zeros((8, 128), F32)] * 3
             if not last:
 
@@ -506,19 +532,24 @@
                 def _(there=there):
                     there.sent()
 
-            def local(e, c=c, totals=totals, here=here):
-                v = basis[j + 1, c, planes(e)] + free[planes(e)] * halo(
-                    here.receive, here.corner_receive, e
-                )
-                basis[j + 1, c, planes(e)] = v
-                weighted = v * part[...]
-                totals[0] = totals[0] + tile_sum(weighted * v)
-                totals[1] = totals[1] + tile_sum(weighted * basis[j, c, planes(e)])
-                lap = laplace(v.reshape(128, 128)).reshape(8, LY, 128)
-                w = mass[...] * lap + minv[c // 3, planes(e)] * v
-                if last:
-                    totals[2] = totals[2] + tile_sum(w * v)
-                return w
+            def local(es, c=c, totals=totals, here=here):
+                blocks = []
+                for e in es:
+                    v = basis[j + 1, c, planes(e)] + free[planes(e)] * halo(
+                        here.receive, here.corner_receive, e
+                    )
+                    basis[j + 1, c, planes(e)] = v
+                    weighted = v * part[...]
+                    totals[0] = totals[0] + tile_sum(weighted * v)
+                    totals[1] = totals[1] + tile_sum(weighted * basis[j, c, planes(e)])
+                    blocks.append(v)
+                out = []
+                for e, v, lap in zip(es, blocks, laplace(blocks)):
+                    w = mass[...] * lap + minv[c // 3, planes(e)] * v
+                    if last:
+                        totals[2] = totals[2] + tile_sum(w * v)
+                    out.append(w)
+                return out
 
             def emit(e, w, c=c, there=there):
                 basis[j + 2, c, planes(e)] = (
@@ -529,10 +560,10 @@
                 there.rows(e, w)
 
             if last:
-                for e in range(ELEMENTS):
-                    local(e)
+                for es in ((0, 3), (1, 2)):
+                    local(es)
             else:
-                assembled(local, emit, there.ends, there.done)
+                assembled(local, emit, there.ends, there.done, gate)
             record(4 * j + c, totals[0])
             record(4 * (ITERS + j) + c, totals[1])
             if last:
@@ -548,6 +579,7 @@
     krylov(jnp.int32(ITERS - 1), True)
 
     value = jnp.sum(macc[...], axis=0, keepdims=True)
+    posted = []
     for k, partners in enumerate(stages):
         arow[k] = value
         copies = []
@@ -568,8 +600,7 @@
             copy.wait_recv()
         for mask, _ in partners:
             value = value + arcv[k, mask]
-        for copy in copies:
-            copy.wait_send()
+        posted.extend(copies)
 
     def moment(index):
         return value if index == 0 else pltpu.roll(value, 128 - 4 * index, 1)
@@ -653,12 +684,12 @@
                 total = term if total is None else total + term
         hcsum[k] = total
 
-    def local_source(e):
-        total = None
+    def local_source(es):
+        totals = None
         for c in range(3):
-            term = divergence(c, fields[c, planes(e)].reshape(128, 128))
-            total = term if total is None else total + term
-        return mass[...] * total.reshape(8, LY, 128)
+            terms = divergence(c, [fields[c, planes(e)] for e in es])
+            totals = terms if totals is None else [a + b for a, b in zip(totals, terms)]
+        return [mass[...] * total for total in totals]
 
     def emit_source(e, w):
         left = -free[planes(e)] * (w + halo(hsum, hcsum, e))
@@ -675,7 +706,7 @@
         assembled(local, emit, faces.ends, faces.done)
 
     assembled(local_source, emit_source)
-    apply_pressure(lambda e: operator(upd[planes(e)]), pressure_faces(0))
+    apply_pressure(lambda es: operator([upd[planes(e)] for e in es]), pressure_faces(0))
     combine(3, coefficients(3))
 
     def refreshed(e, faces, keep, gain):
@@ -699,11 +730,14 @@
         def _():
             there.sent()
 
-        def local(e):
-            left, update = refreshed(e, here, keep, gain)
-            rem[planes(e)] = left
-            upd[planes(e)] = update
-            return operator(update)
+        def local(es):
+            updates = []
+            for e in es:
+                left, update = refreshed(e, here, keep, gain)
+                rem[planes(e)] = left
+                upd[planes(e)] = update
+                updates.append(update)
+            return operator(updates)
 
         apply_pressure(local, there)
         return carry
@@ -713,6 +747,8 @@
     here.arrived()
     for e in range(ELEMENTS):
         refreshed(e, here, pairs[CHEB - 1][0], pairs[CHEB - 1][1])
+    for copy in posted:
+        copy.wait_send()
     for slot in range(2):
         pressure_faces(slot).sent()
         for c in range(4):

time: 81.3 us -> 80.6 us (level)
  no operation moved by 1% of the time
where the time goes in v4:
time: 80.6 us; the launch traced here: 80.5 us
  Pallas kernels  79.8 us (99%)
    pallas_call x1, Pallas kernels, on_device(): pl.pallas_call(body, out_shape=(pltpu.VMEM((4,) + brick, F32), pltpu.VMEM...  78.8 us

profile of v4, /device:TPU:1, one launch (start us, length us, event | category | flops | bytes accessed | tf_op | source)
XLA Modules:
  0.0 80.5 jit_solution(15247846103628691689)
XLA Ops:
  0.6 78.8 %shard_map.68 = (f32[4,32,16,128]{3,2,1,0:T(8,128)S(1)}, f32[32,16,128]{2,1,0:T(8,128)S(1)}) custom-call(f32[4,32,16,128]{3,2,1,0:T(8,128)} %refs_0_.1, f32[32,16,128]{2,1,0:T(8,128)} %refs_1_.1, s32[32,16,128]{2,1,0:T(8,128)} %refs_2_.1, bf16[4,256,256]{2,1,0:T(8,128)(2,1)} %constant.4.clone.refs_3_, f32[3,8,16,128]{3,2,1,0:T(8,128)} %constant.5.clone.refs_4_), custom_call_target="tpu_custom_call" | custom-call | tf_op jit(solution)/shard_map/pallas_call | solution.py:786
  79.4 1.1 %shard_map.69 = (f32[4,32,16,128]{3,2,1,0:T(8,128)}, f32[32,16,128]{2,1,0:T(8,128)}) custom-call(f32[4,32,16,128]{3,2,1,0:T(8,128)S(1)} %get-tuple-element.4.fields, f32[32,16,128]{2,1,0:T(8,128)S(1)} %get-tuple-element.5.pressure), custom_call_target="tpu_custom_call" | custom-call | tf_op jit(solution)/shard_map/pallas_call | solution.py:831

commit v5 on v4

--- a/solution.py
+++ b/solution.py
@@ -167,10 +167,10 @@
 
 def step_kernel(nx, ny, *refs):
     (old_hbm, inv_hbm, bnd_hbm, mat_hbm, tab_hbm, fields, prs) = refs[:7]
-    (old, inv, bnd, mat_ref, tab_ref, free, minv, basis, rem, upd) = refs[7:17]
-    (vsnd, vrcv, vcsnd, vcrcv, psnd, prcv, pcsnd, pcrcv) = refs[17:25]
-    (ssnd, srcv, scsnd, scrcv, hsum, hcsum, macc, arow, arcv) = refs[25:34]
-    (lsem, vsem, psem, ssem, ass, ars) = refs[34:]
+    (old, inv, bnd, mat_ref, tab_ref, free, minv, basis, parts, rem, upd) = refs[7:18]
+    (vsnd, vrcv, vcsnd, vcrcv, psnd, prcv, pcsnd, pcrcv) = refs[18:26]
+    (ssnd, srcv, scsnd, scrcv, hsum, hcsum, macc, arow, arcv) = refs[26:35]
+    (lsem, vsem, psem, ssem, ass, ars) = refs[35:]
 
     gx = lax.axis_index("gx")
     gy = lax.axis_index("gy")
@@ -511,7 +511,11 @@
                 blocks = [basis[j + 1, c, planes(e)] for e in es]
                 return [mass[...] * out for out in divergence(c, blocks)]
 
-            assembled(local, faces.rows, faces.keep_ends)
+            def emit(e, w, c=c, faces=faces):
+                parts[j, c, planes(e)] = w
+                faces.rows(e, w)
+
+            assembled(local, emit, faces.keep_ends)
         group.post_all()
 
     def krylov(j, last):
@@ -664,9 +668,6 @@
                 fields[c, where[0], where[1]] = total
 
     known = [coefficients(c) for c in range(3)]
-    for c in range(3):
-        combine(c, known[c])
-
     for j in range(ITERS):
         source_faces(j).arrived()
     for r in range(0, FACE_ROWS, 8):
@@ -684,19 +685,20 @@
                 total = term if total is None else total + term
         hcsum[k] = total
 
-    def local_source(es):
-        totals = None
-        for c in range(3):
-            terms = divergence(c, [fields[c, planes(e)] for e in es])
-            totals = terms if totals is None else [a + b for a, b in zip(totals, terms)]
-        return [mass[...] * total for total in totals]
-
-    def emit_source(e, w):
-        left = -free[planes(e)] * (w + halo(hsum, hcsum, e))
-        update = pairs[0][1] * (invd[...] * left)
-        rem[planes(e)] = left
-        upd[planes(e)] = update
-        prs[planes(e)] = update
+    for e in range(ELEMENTS):
+        border = halo(hsum, hcsum, e)
+        for x in range(8):
+            for y in (0, 8):
+                where = (8 * e + x, pl.ds(y, 8))
+                total = border[x, y : y + 8]
+                for c in range(3):
+                    for j in range(ITERS):
+                        total = total + known[c][j][0] * parts[j, c, where[0], where[1]]
+                left = -free[where[0], where[1]] * total
+                update = pairs[0][1] * (invd[x, pl.ds(y, 8)] * left)
+                rem[where[0], where[1]] = left
+                upd[where[0], where[1]] = update
+                prs[where[0], where[1]] = update
 
     def apply_pressure(local, faces):
         def emit(e, w):
@@ -705,8 +707,9 @@
 
         assembled(local, emit, faces.ends, faces.done)
 
-    assembled(local_source, emit_source)
     apply_pressure(lambda es: operator([upd[planes(e)] for e in es]), pressure_faces(0))
+    for c in range(3):
+        combine(c, known[c])
     combine(3, coefficients(3))
 
     def refreshed(e, faces, keep, gain):
@@ -797,6 +800,7 @@
                 pltpu.VMEM(brick, F32),
                 pltpu.VMEM((2,) + brick, F32),
                 pltpu.VMEM((ITERS + 1, 4) + brick, F32),
+                pltpu.VMEM((ITERS, 3) + brick, F32),
                 pltpu.VMEM(brick, F32),
                 pltpu.VMEM(brick, F32),
                 pltpu.VMEM((2, 4, FACE_ROWS, 128), F32),

time: 80.6 us -> 80.3 us (level)
  no operation moved by 1% of the time
where the time goes in v5:
time: 80.3 us; the launch traced here: 80.2 us
  Pallas kernels  79.5 us (99%)
    pallas_call x1, Pallas kernels, on_device(): pl.pallas_call(body, out_shape=(pltpu.VMEM((4,) + brick, F32), pltpu.VMEM...  78.4 us

profile of v5, /device:TPU:1, one launch (start us, length us, event | category | flops | bytes accessed | tf_op | source)
XLA Modules:
  0.0 80.2 jit_solution(16075680611156436194)
XLA Ops:
  0.6 78.4 %shard_map.68 = (f32[4,32,16,128]{3,2,1,0:T(8,128)S(1)}, f32[32,16,128]{2,1,0:T(8,128)S(1)}) custom-call(f32[4,32,16,128]{3,2,1,0:T(8,128)} %refs_0_.1, f32[32,16,128]{2,1,0:T(8,128)} %refs_1_.1, s32[32,16,128]{2,1,0:T(8,128)} %refs_2_.1, bf16[4,256,256]{2,1,0:T(8,128)(2,1)} %constant.4.clone.refs_3_, f32[3,8,16,128]{3,2,1,0:T(8,128)} %constant.5.clone.refs_4_), custom_call_target="tpu_custom_call" | custom-call | tf_op jit(solution)/shard_map/pallas_call | solution.py:789
  79.1 1.1 %shard_map.69 = (f32[4,32,16,128]{3,2,1,0:T(8,128)}, f32[32,16,128]{2,1,0:T(8,128)}) custom-call(f32[4,32,16,128]{3,2,1,0:T(8,128)S(1)} %get-tuple-element.4.fields, f32[32,16,128]{2,1,0:T(8,128)S(1)} %get-tuple-element.5.pressure), custom_call_target="tpu_custom_call" | custom-call | tf_op jit(solution)/shard_map/pallas_call | solution.py:835

commit v6 on v5

--- a/solution.py
+++ b/solution.py
@@ -746,18 +746,22 @@
         return carry
 
     lax.fori_loop(1, CHEB - 1, chebyshev_body, 0)
-    here = pressure_faces(CHEB % 2)
-    here.arrived()
-    for e in range(ELEMENTS):
-        refreshed(e, here, pairs[CHEB - 1][0], pairs[CHEB - 1][1])
     for copy in posted:
         copy.wait_send()
     for slot in range(2):
-        pressure_faces(slot).sent()
         for c in range(4):
             velocity_faces(slot, c).sent()
     for j in range(ITERS):
         source_faces(j).sent()
+    pressure_faces(CHEB % 2 + 1).sent()
+    here = pressure_faces(CHEB % 2)
+    here.sent()
+    here.faces_arrived()
+    for e in (1, 2):
+        refreshed(e, here, pairs[CHEB - 1][0], pairs[CHEB - 1][1])
+    here.corners_arrived()
+    for e in (0, 3):
+        refreshed(e, here, pairs[CHEB - 1][0], pairs[CHEB - 1][1])
 
 
 def store_kernel(fields, pressure, new_hbm, prs_hbm, sems):

time: 80.3 us -> 80.1 us (level)
  no operation moved by 1% of the time
where the time goes in v6:
time: 80.1 us; the launch traced here: 80 us
  Pallas kernels  79.4 us (99%)
    pallas_call x1, Pallas kernels, on_device(): pl.pallas_call(body, out_shape=(pltpu.VMEM((4,) + brick, F32), pltpu.VMEM...  78.3 us

profile of v6, /device:TPU:1, one launch (start us, length us, event | category | flops | bytes accessed | tf_op | source)
XLA Modules:
  0.0 80.0 jit_solution(5675237544308251337)
XLA Ops:
  0.6 78.3 %shard_map.68 = (f32[4,32,16,128]{3,2,1,0:T(8,128)S(1)}, f32[32,16,128]{2,1,0:T(8,128)S(1)}) custom-call(f32[4,32,16,128]{3,2,1,0:T(8,128)} %refs_0_.1, f32[32,16,128]{2,1,0:T(8,128)} %refs_1_.1, s32[32,16,128]{2,1,0:T(8,128)} %refs_2_.1, bf16[4,256,256]{2,1,0:T(8,128)(2,1)} %constant.4.clone.refs_3_, f32[3,8,16,128]{3,2,1,0:T(8,128)} %constant.5.clone.refs_4_), custom_call_target="tpu_custom_call" | custom-call | tf_op jit(solution)/shard_map/pallas_call | solution.py:793
  78.9 1.1 %shard_map.69 = (f32[4,32,16,128]{3,2,1,0:T(8,128)}, f32[32,16,128]{2,1,0:T(8,128)}) custom-call(f32[4,32,16,128]{3,2,1,0:T(8,128)S(1)} %get-tuple-element.4.fields, f32[32,16,128]{2,1,0:T(8,128)S(1)} %get-tuple-element.5.pressure), custom_call_target="tpu_custom_call" | custom-call | tf_op jit(solution)/shard_map/pallas_call | solution.py:839
